TPU v7x, 512 devices: a whole 4x8x8 slice. The times are simulated.
512 devices in a mesh: tm: 16 (over y_hi, z), gz: 32 (over y_lo, x, core).
Axes of the slice: x: 4, y: 8 (y_hi: 2, y_lo: 4; y = y_hi * 4 + y_lo), z: 8, core: 2. Of those that a mesh axis runs over, the one named last changes fastest.
Arguments:
- starts: float32 [16, 128, 128, 128], P('tm', 'gz'), may hold values from -6 to 6
- materials: int32 [128, 128, 128], P('gz'), may hold values from 0 to 2
- conductivity: float32 [3], replicated, may hold values from 0.4 to 2.5
- pre_factor: float32 [3], replicated, may hold values from 0.2 to 1
- activation: float32 [3], replicated, may hold values from 0.5 to 1.5
Outputs:
- next_starts: float32 [16, 128, 128, 128], P('tm', 'gz')
Inputs may be any that keep to these rules, and one draw needn't show every extreme that they name: `materials`: material ids: 0 cell, 1 coolant, 2 casing.
All inputs are finite; a program needn't handle non-finite values.
Results may differ from a plain program's by a relative error of at most 0.0001.
Values sent between devices are 32-bit elements; how exact they have to be, the bound alone decides.
A program may use at most 128 MiB of HBM per device.

v0:
```python
import jax
import jax.numpy as jnp
from jax import lax
from jax.sharding import PartitionSpec as P

FSTEPS = 4
CSTEPS = 1


step_size = 0.06


def with_halo(block, sides, width):
    for axis, dim in sides:
        count = lax.axis_size(axis)
        forward = [(i, i + 1) for i in range(count - 1)]
        backward = [(target, source) for source, target in forward]
        low = lax.ppermute(
            lax.slice_in_dim(block, block.shape[dim] - width, None, axis=dim), axis, forward
        )
        high = lax.ppermute(lax.slice_in_dim(block, 0, width, axis=dim), axis, backward)
        block = jnp.concatenate([low, block, high], axis=dim)
    return block


def passed_along(block, axis, distance):
    devices = range(lax.axis_size(axis))
    route = [(i - distance, i) for i in devices if i - distance in devices]
    return lax.ppermute(block, axis, route)


def lookup(identity, table):
    total = jnp.zeros(identity.shape, jnp.float32)
    for index in range(3):
        total = total + jnp.where(identity == index, table[index], jnp.float32(0.0))
    return total


def heat_step(padded, conduct, source_pre, source_act, step_dt, inv_area):
    centre = padded[1:-1, 1:-1, 1:-1]
    cond_centre = conduct[1:-1, 1:-1, 1:-1]
    windows = [
        (slice(2, None), slice(1, -1), slice(1, -1)),
        (slice(None, -2), slice(1, -1), slice(1, -1)),
        (slice(1, -1), slice(2, None), slice(1, -1)),
        (slice(1, -1), slice(None, -2), slice(1, -1)),
        (slice(1, -1), slice(1, -1), slice(2, None)),
        (slice(1, -1), slice(1, -1), slice(None, -2)),
    ]
    total = jnp.zeros(centre.shape, jnp.float32)
    for window in windows:
        total = total + 0.5 * (cond_centre + conduct[window]) * (padded[window] - centre)
    release = source_pre * jnp.exp(source_act * centre / (1.0 + jnp.abs(centre)))
    return centre + step_dt * (inv_area * total + release)


def down(field):
    depth, width, height = field.shape
    return field.reshape(depth // 4, 4, width // 4, 4, height // 4, 4).mean(axis=(1, 3, 5))


def up(field):
    return jnp.repeat(jnp.repeat(jnp.repeat(field, 4, 0), 4, 1), 4, 2)


def pad_sides(field):
    return jnp.pad(field, ((0, 0), (1, 1), (1, 1)))


def on_device(starts, materials, conductivity, pre_factor, activation):
    field_start = starts[0]
    slab_cells = field_start.shape[0]
    n_slabs = lax.axis_size("gz")
    n_slices = lax.axis_size("tm")
    slab_index = lax.axis_index("gz")
    slice_index = lax.axis_index("tm")
    coarse_dt = step_size * FSTEPS / CSTEPS
    margin = FSTEPS
    ids_ext = with_halo(materials, (("gz", 0),), FSTEPS)
    cond_all = lookup(pad_sides(ids_ext), conductivity)
    pre_all = lookup(ids_ext, pre_factor)
    act_all = lookup(ids_ext, activation)
    positions = (
        slab_index * slab_cells + jnp.arange(slab_cells + 2 * margin, dtype=jnp.int32) - margin
    )
    inside = ((positions >= 0) & (positions < slab_cells * n_slabs)).astype(jnp.float32)
    fine_field = field_start
    for step in range(FSTEPS):
        extended = with_halo(fine_field, (("gz", 0),), 1)
        length = extended.shape[0]
        lower = margin - 1
        stepped = heat_step(
            pad_sides(extended),
            cond_all[lower : lower + length],
            pre_all[lower + 1 : lower + length - 1],
            act_all[lower + 1 : lower + length - 1],
            step_size,
            1.0,
        )
        fine_field = stepped * inside[lower + 1 : lower + length - 1][:, None, None]
    cond_coarse_ext = down(cond_all[margin - 4 : margin + slab_cells + 4, 1:-1, 1:-1])
    cond_coarse_pad = jnp.pad(
        cond_coarse_ext, ((0, 0), (1, 1), (1, 1)), constant_values=conductivity[0]
    )
    pre_coarse = down(pre_all[margin : margin + slab_cells])
    act_coarse = down(act_all[margin : margin + slab_cells])

    def coarse_sharded(state):
        extended = with_halo(state, (("gz", 0),), 1)
        state = heat_step(
            pad_sides(extended), cond_coarse_pad, pre_coarse, act_coarse, coarse_dt, 1.0 / 16.0
        )
        return state

    own_coarse = down(field_start)
    old_coarse = coarse_sharded(own_coarse)
    diff = fine_field - up(old_coarse)
    prev_diff = passed_along(diff, "tm", 1)
    coarse_prev = down(prev_diff)

    def link(counter, carry):
        state, latest = carry
        received = passed_along(state, "tm", 1)
        latest = coarse_sharded(received)
        state = jnp.where(slice_index == 0, own_coarse, latest + coarse_prev)
        return (state, latest)

    final_state, latest = lax.fori_loop(0, n_slices, link, (own_coarse, jnp.zeros_like(own_coarse)))
    result = jnp.where(slice_index == 0, field_start, up(latest) + prev_diff)
    return result[None]


def solution(mesh):
    return jax.shard_map(
        on_device,
        mesh=mesh,
        in_specs=(P("tm", "gz", None, None), P("gz", None, None), P(), P(), P()),
        out_specs=P("tm", "gz", None, None),
        check_vma=False,
    )
```

profile of v0, /device:TPU:56, one launch (start us, length us, event | category | flops | bytes accessed | tf_op | source)
XLA Modules:
  0.0 503.0 jit_solution(6295417498029489502)
XLA Ops:
  1.9 5.8 %collective-permute-start.4 = (s32[4,128,128]{2,1,0:T(8,128)}, s32[4,128,128]{2,1,0:T(8,128)S(1)}, u32[]{:S(2)}, u32[]{:S(2)}) collective-permute-start(s32[4,128,128]{2,1,0:T(8,128)} %param.8), channel_id=1, source_target_pairs={{1,0},{2,1},{3,2},{4,3},{5,4},{6,5},{7,6},{8,7},{9,8},{10,9},{11,1... | collective-permute-start | bytes 786440 | tf_op jit(solution)/shard_map/ppermute | solution.py:21
  24.9 5.6 %collective-permute-done.6 = f32[1,128,128]{2,1,0:T(8,128)S(1)} collective-permute-done((f32[1,128,128]{2,1,0:T(8,128)S(1)}, f32[1,128,128]{2,1,0:T(8,128)S(1)}, u32[]{:S(2)}, u32[]{:S(2)}) %collective-permute-start.6) | collective-permute-done | bytes 65568 | tf_op jit(solution)/shard_map/ppermute | solution.py:18
  35.6 28.2 %reshape.138 = f32[3,4,32,4,32,4]{5,4,3,2,1,0:T(8,128)} reshape(f32[12,128,128]{2,1,0:T(8,128)} %slice.399) | data formatting | bytes 1572864 | tf_op jit(solution)/shard_map/reshape | solution.py:59
  63.8 10.0 %reduce_sum.60 = f32[3,32,32]{2,1,0:T(8,128)} reduce(f32[3,4,32,4,32,4]{5,4,3,2,1,0:T(8,128)} %reshape.138, f32[]{:T(128)} %constant.73.clone.1), dimensions={1,3,5}, to_apply=%region_6.7 | reduce | flops 193536 | bytes 798724 | tf_op jit(solution)/shard_map/reduce_sum | solution.py:59
  96.1 5.8 %collective-permute-start.9 = (f32[1,128,128]{2,1,0:T(8,128)}, f32[1,128,128]{2,1,0:T(8,128)}, u32[]{:S(2)}, u32[]{:S(2)}) collective-permute-start(f32[1,128,128]{2,1,0:T(8,128)} %get-tuple-element.196), channel_id=1, source_target_pairs={{1,0},{2,1},{3,2},{4,3},{5,4},{6,5},{7,6},{8,7},{9,8},{10,9},{11,1... | collective-permute-start | bytes 196616 | tf_op jit(solution)/shard_map/ppermute | solution.py:21
  114.0 5.6 %fusion.41 = f32[4,128,128]{2,1,0:T(8,128)S(1)} fusion(f32[4,128,128]{2,1,0:T(8,128)} %copy-done.11, f32[4,128,128]{2,1,0:T(8,128)} %copy-done.9, f32[6,130,130]{2,1,0:T(8,128)S(1)} %select_maximum_fusion.4, f32[4,128,128]{2,1,0:T(8,128)} %copy-done.7, f32[4,128,128]{2,1,0:T(8,128)S(1)} %copy-done.6, f32[4,128,128]{2,1,0:T(8,128)S(1)} %copy-done.4, ...), kind=kLoop, calls=%fused_computation.78 | loop fusion | flops 2490368 | bytes 3473448 | tf_op jit(solution)/shard_map/mul | solution.py:100
  139.1 13.3 %collective-permute-done.15 = f32[4,128,128]{2,1,0:T(8,128)S(1)} collective-permute-done((f32[4,128,128]{2,1,0:T(8,128)S(1)}, f32[4,128,128]{2,1,0:T(8,128)S(1)}, u32[]{:S(2)}, u32[]{:S(2)}) %collective-permute-start.15) | collective-permute-done | bytes 262176 | tf_op jit(solution)/shard_map/ppermute | solution.py:29
  154.9 346.5 %while.17 = (s32[]{:T(128)}, f32[1,32,32]{2,1,0:T(8,128)S(1)}, f32[1,32,32]{2,1,0:T(8,128)}, pred[]{:T(512)}, f32[1,32,32]{2,1,0:T(8,128)S(1)}, /*index=5*/f32[1...) while((s32[]{:T(128)}, f32[1,32,32]{2,1,0:T(8,128)S(1)}, ...), condition=%wide.region_10.11_spmd, body=%wide.region_9.10_spmd.sunk | while | flops 86838 | bytes 153398 | solution.py:128
  156.8 9.7 %collective-permute-done = f32[1,32,32]{2,1,0:T(8,128)S(1)} collective-permute-done((f32[1,32,32]{2,1,0:T(8,128)S(1)}, f32[1,32,32]{2,1,0:T(8,128)S(1)}, u32[]{:S(2)}, u32[]{:S(2)}) %collective-permute-start) | collective-permute-done | bytes 4128 | tf_op jit(solution)/shard_map/while/body/eval_jaxpr/ppermute | solution.py:29
  180.5 9.7 %collective-permute-done = f32[1,32,32]{2,1,0:T(8,128)S(1)} collective-permute-done((f32[1,32,32]{2,1,0:T(8,128)S(1)}, f32[1,32,32]{2,1,0:T(8,128)S(1)}, u32[]{:S(2)}, u32[]{:S(2)}) %collective-permute-start) | collective-permute-done | bytes 4128 | tf_op jit(solution)/shard_map/while/body/eval_jaxpr/ppermute | solution.py:29
  202.0 9.7 %collective-permute-done = f32[1,32,32]{2,1,0:T(8,128)S(1)} collective-permute-done((f32[1,32,32]{2,1,0:T(8,128)S(1)}, f32[1,32,32]{2,1,0:T(8,128)S(1)}, u32[]{:S(2)}, u32[]{:S(2)}) %collective-permute-start) | collective-permute-done | bytes 4128 | tf_op jit(solution)/shard_map/while/body/eval_jaxpr/ppermute | solution.py:29
  223.5 9.7 %collective-permute-done = f32[1,32,32]{2,1,0:T(8,128)S(1)} collective-permute-done((f32[1,32,32]{2,1,0:T(8,128)S(1)}, f32[1,32,32]{2,1,0:T(8,128)S(1)}, u32[]{:S(2)}, u32[]{:S(2)}) %collective-permute-start) | collective-permute-done | bytes 4128 | tf_op jit(solution)/shard_map/while/body/eval_jaxpr/ppermute | solution.py:29
  245.0 9.7 %collective-permute-done = f32[1,32,32]{2,1,0:T(8,128)S(1)} collective-permute-done((f32[1,32,32]{2,1,0:T(8,128)S(1)}, f32[1,32,32]{2,1,0:T(8,128)S(1)}, u32[]{:S(2)}, u32[]{:S(2)}) %collective-permute-start) | collective-permute-done | bytes 4128 | tf_op jit(solution)/shard_map/while/body/eval_jaxpr/ppermute | solution.py:29
  266.6 9.7 %collective-permute-done = f32[1,32,32]{2,1,0:T(8,128)S(1)} collective-permute-done((f32[1,32,32]{2,1,0:T(8,128)S(1)}, f32[1,32,32]{2,1,0:T(8,128)S(1)}, u32[]{:S(2)}, u32[]{:S(2)}) %collective-permute-start) | collective-permute-done | bytes 4128 | tf_op jit(solution)/shard_map/while/body/eval_jaxpr/ppermute | solution.py:29
  288.1 9.7 %collective-permute-done = f32[1,32,32]{2,1,0:T(8,128)S(1)} collective-permute-done((f32[1,32,32]{2,1,0:T(8,128)S(1)}, f32[1,32,32]{2,1,0:T(8,128)S(1)}, u32[]{:S(2)}, u32[]{:S(2)}) %collective-permute-start) | collective-permute-done | bytes 4128 | tf_op jit(solution)/shard_map/while/body/eval_jaxpr/ppermute | solution.py:29
  309.6 9.7 %collective-permute-done = f32[1,32,32]{2,1,0:T(8,128)S(1)} collective-permute-done((f32[1,32,32]{2,1,0:T(8,128)S(1)}, f32[1,32,32]{2,1,0:T(8,128)S(1)}, u32[]{:S(2)}, u32[]{:S(2)}) %collective-permute-start) | collective-permute-done | bytes 4128 | tf_op jit(solution)/shard_map/while/body/eval_jaxpr/ppermute | solution.py:29
  331.1 9.7 %collective-permute-done = f32[1,32,32]{2,1,0:T(8,128)S(1)} collective-permute-done((f32[1,32,32]{2,1,0:T(8,128)S(1)}, f32[1,32,32]{2,1,0:T(8,128)S(1)}, u32[]{:S(2)}, u32[]{:S(2)}) %collective-permute-start) | collective-permute-done | bytes 4128 | tf_op jit(solution)/shard_map/while/body/eval_jaxpr/ppermute | solution.py:29
  352.6 9.7 %collective-permute-done = f32[1,32,32]{2,1,0:T(8,128)S(1)} collective-permute-done((f32[1,32,32]{2,1,0:T(8,128)S(1)}, f32[1,32,32]{2,1,0:T(8,128)S(1)}, u32[]{:S(2)}, u32[]{:S(2)}) %collective-permute-start) | collective-permute-done | bytes 4128 | tf_op jit(solution)/shard_map/while/body/eval_jaxpr/ppermute | solution.py:29
  374.1 9.7 %collective-permute-done = f32[1,32,32]{2,1,0:T(8,128)S(1)} collective-permute-done((f32[1,32,32]{2,1,0:T(8,128)S(1)}, f32[1,32,32]{2,1,0:T(8,128)S(1)}, u32[]{:S(2)}, u32[]{:S(2)}) %collective-permute-start) | collective-permute-done | bytes 4128 | tf_op jit(solution)/shard_map/while/body/eval_jaxpr/ppermute | solution.py:29
  395.7 9.7 %collective-permute-done = f32[1,32,32]{2,1,0:T(8,128)S(1)} collective-permute-done((f32[1,32,32]{2,1,0:T(8,128)S(1)}, f32[1,32,32]{2,1,0:T(8,128)S(1)}, u32[]{:S(2)}, u32[]{:S(2)}) %collective-permute-start) | collective-permute-done | bytes 4128 | tf_op jit(solution)/shard_map/while/body/eval_jaxpr/ppermute | solution.py:29
  417.2 9.7 %collective-permute-done = f32[1,32,32]{2,1,0:T(8,128)S(1)} collective-permute-done((f32[1,32,32]{2,1,0:T(8,128)S(1)}, f32[1,32,32]{2,1,0:T(8,128)S(1)}, u32[]{:S(2)}, u32[]{:S(2)}) %collective-permute-start) | collective-permute-done | bytes 4128 | tf_op jit(solution)/shard_map/while/body/eval_jaxpr/ppermute | solution.py:29
  438.7 9.7 %collective-permute-done = f32[1,32,32]{2,1,0:T(8,128)S(1)} collective-permute-done((f32[1,32,32]{2,1,0:T(8,128)S(1)}, f32[1,32,32]{2,1,0:T(8,128)S(1)}, u32[]{:S(2)}, u32[]{:S(2)}) %collective-permute-start) | collective-permute-done | bytes 4128 | tf_op jit(solution)/shard_map/while/body/eval_jaxpr/ppermute | solution.py:29
  460.2 9.7 %collective-permute-done = f32[1,32,32]{2,1,0:T(8,128)S(1)} collective-permute-done((f32[1,32,32]{2,1,0:T(8,128)S(1)}, f32[1,32,32]{2,1,0:T(8,128)S(1)}, u32[]{:S(2)}, u32[]{:S(2)}) %collective-permute-start) | collective-permute-done | bytes 4128 | tf_op jit(solution)/shard_map/while/body/eval_jaxpr/ppermute | solution.py:29
  481.7 9.7 %collective-permute-done = f32[1,32,32]{2,1,0:T(8,128)S(1)} collective-permute-done((f32[1,32,32]{2,1,0:T(8,128)S(1)}, f32[1,32,32]{2,1,0:T(8,128)S(1)}, u32[]{:S(2)}, u32[]{:S(2)}) %collective-permute-start) | collective-permute-done | bytes 4128 | tf_op jit(solution)/shard_map/while/body/eval_jaxpr/ppermute | solution.py:29
  (242 shorter events, 271.7 us)
Async XLA Ops:
  0.0 30.8 %collective-permute-start.3 = (s32[4,128,128]{2,1,0:T(8,128)}, s32[4,128,128]{2,1,0:T(8,128)S(1)}, u32[]{:S(2)}, u32[]{:S(2)}) collective-permute-start(s32[4,128,128]{2,1,0:T(8,128)} %param.8), channel_id=1, source_target_pairs={{0,1},{1,2},{2,3},{3,4},{4,5},{5,6},{6,7},{7,8},{8,9},{9,10},{10,1... | collective-permute-start | bytes 786440 | tf_op jit(solution)/shard_map/ppermute | solution.py:18
  1.9 29.0 %collective-permute-start.4 = (s32[4,128,128]{2,1,0:T(8,128)}, s32[4,128,128]{2,1,0:T(8,128)S(1)}, u32[]{:S(2)}, u32[]{:S(2)}) collective-permute-start(s32[4,128,128]{2,1,0:T(8,128)} %param.8), channel_id=1, source_target_pairs={{1,0},{2,1},{3,2},{4,3},{5,4},{6,5},{7,6},{8,7},{9,8},{10,9},{11,1... | collective-permute-start | bytes 786440 | tf_op jit(solution)/shard_map/ppermute | solution.py:21
  11.1 11.7 %collective-permute-start.13 = (f32[1,32,32]{2,1,0:T(8,128)S(1)}, f32[1,32,32]{2,1,0:T(8,128)S(1)}, u32[]{:S(2)}, u32[]{:S(2)}) collective-permute-start(f32[1,32,32]{2,1,0:T(8,128)S(1)} %multiply_bitcast_fusion.3), channel_id=1, source_target_pairs={{1,0},{2,1},{3,2},{4,3},{5,4},{6,5},{7,6},{8,7},{9,8},{10,9},{11,1... | collective-permute-start | bytes 12296 | tf_op jit(solution)/shard_map/ppermute | solution.py:21
  13.0 11.7 %collective-permute-start.14 = (f32[1,32,32]{2,1,0:T(8,128)S(1)}, f32[1,32,32]{2,1,0:T(8,128)S(1)}, u32[]{:S(2)}, u32[]{:S(2)}) collective-permute-start(f32[1,32,32]{2,1,0:T(8,128)S(1)} %multiply_bitcast_fusion.3), channel_id=1, source_target_pairs={{0,1},{1,2},{2,3},{3,4},{4,5},{5,6},{6,7},{7,8},{8,9},{9,10},{10,1... | collective-permute-start | bytes 12296 | tf_op jit(solution)/shard_map/ppermute | solution.py:18
  22.8 7.7 %collective-permute-start.6 = (f32[1,128,128]{2,1,0:T(8,128)S(1)}, f32[1,128,128]{2,1,0:T(8,128)S(1)}, u32[]{:S(2)}, u32[]{:S(2)}) collective-permute-start(f32[1,128,128]{2,1,0:T(8,128)S(1)} %get-tuple-element.199), channel_id=1, source_target_pairs={{0,1},{1,2},{2,3},{3,4},{4,5},{5,6},{6,7},{7,8},{8,9},{9,10},{10,1... | collective-permute-start | bytes 196616 | tf_op jit(solution)/shard_map/ppermute | solution.py:18
  94.2 18.4 %collective-permute-start.10 = (f32[1,128,128]{2,1,0:T(8,128)}, f32[1,128,128]{2,1,0:T(8,128)}, u32[]{:S(2)}, u32[]{:S(2)}) collective-permute-start(f32[1,128,128]{2,1,0:T(8,128)} %get-tuple-element.195), channel_id=1, source_target_pairs={{0,1},{1,2},{2,3},{3,4},{4,5},{5,6},{6,7},{7,8},{8,9},{9,10},{10,1... | collective-permute-start | bytes 196616 | tf_op jit(solution)/shard_map/ppermute | solution.py:18
  96.1 16.5 %collective-permute-start.9 = (f32[1,128,128]{2,1,0:T(8,128)}, f32[1,128,128]{2,1,0:T(8,128)}, u32[]{:S(2)}, u32[]{:S(2)}) collective-permute-start(f32[1,128,128]{2,1,0:T(8,128)} %get-tuple-element.196), channel_id=1, source_target_pairs={{1,0},{2,1},{3,2},{4,3},{5,4},{6,5},{7,6},{8,7},{9,8},{10,9},{11,1... | collective-permute-start | bytes 196616 | tf_op jit(solution)/shard_map/ppermute | solution.py:21
  134.8 17.6 %collective-permute-start.15 = (f32[4,128,128]{2,1,0:T(8,128)S(1)}, f32[4,128,128]{2,1,0:T(8,128)S(1)}, u32[]{:S(2)}, u32[]{:S(2)}) collective-permute-start(f32[4,128,128]{2,1,0:T(8,128)S(1)} %fusion.24), channel_id=1, source_target_pairs={{0,32},{32,64},{64,96},{96,128},{128,160},{160,192},{192,224},{224... | collective-permute-start | bytes 786440 | tf_op jit(solution)/shard_map/ppermute | solution.py:29
  154.9 11.6 %collective-permute-start = (f32[1,32,32]{2,1,0:T(8,128)S(1)}, f32[1,32,32]{2,1,0:T(8,128)S(1)}, u32[]{:S(2)}, u32[]{:S(2)}) collective-permute-start(f32[1,32,32]{2,1,0:T(8,128)S(1)} %get-tuple-element.315), channel_id=1, source_target_pairs={{0,32},{32,64},{64,96},{96,128},{128,160},{160,192},{192,224},{224... | collective-permute-start | bytes 12296 | tf_op jit(solution)/shard_map/while/body/eval_jaxpr/ppermute | solution.py:29
  178.6 11.6 %collective-permute-start = (f32[1,32,32]{2,1,0:T(8,128)S(1)}, f32[1,32,32]{2,1,0:T(8,128)S(1)}, u32[]{:S(2)}, u32[]{:S(2)}) collective-permute-start(f32[1,32,32]{2,1,0:T(8,128)S(1)} %get-tuple-element.315), channel_id=1, source_target_pairs={{0,32},{32,64},{64,96},{96,128},{128,160},{160,192},{192,224},{224... | collective-permute-start | bytes 12296 | tf_op jit(solution)/shard_map/while/body/eval_jaxpr/ppermute | solution.py:29
  200.1 11.6 %collective-permute-start = (f32[1,32,32]{2,1,0:T(8,128)S(1)}, f32[1,32,32]{2,1,0:T(8,128)S(1)}, u32[]{:S(2)}, u32[]{:S(2)}) collective-permute-start(f32[1,32,32]{2,1,0:T(8,128)S(1)} %get-tuple-element.315), channel_id=1, source_target_pairs={{0,32},{32,64},{64,96},{96,128},{128,160},{160,192},{192,224},{224... | collective-permute-start | bytes 12296 | tf_op jit(solution)/shard_map/while/body/eval_jaxpr/ppermute | solution.py:29
  221.6 11.6 %collective-permute-start = (f32[1,32,32]{2,1,0:T(8,128)S(1)}, f32[1,32,32]{2,1,0:T(8,128)S(1)}, u32[]{:S(2)}, u32[]{:S(2)}) collective-permute-start(f32[1,32,32]{2,1,0:T(8,128)S(1)} %get-tuple-element.315), channel_id=1, source_target_pairs={{0,32},{32,64},{64,96},{96,128},{128,160},{160,192},{192,224},{224... | collective-permute-start | bytes 12296 | tf_op jit(solution)/shard_map/while/body/eval_jaxpr/ppermute | solution.py:29
  243.1 11.6 %collective-permute-start = (f32[1,32,32]{2,1,0:T(8,128)S(1)}, f32[1,32,32]{2,1,0:T(8,128)S(1)}, u32[]{:S(2)}, u32[]{:S(2)}) collective-permute-start(f32[1,32,32]{2,1,0:T(8,128)S(1)} %get-tuple-element.315), channel_id=1, source_target_pairs={{0,32},{32,64},{64,96},{96,128},{128,160},{160,192},{192,224},{224... | collective-permute-start | bytes 12296 | tf_op jit(solution)/shard_map/while/body/eval_jaxpr/ppermute | solution.py:29
  264.6 11.6 %collective-permute-start = (f32[1,32,32]{2,1,0:T(8,128)S(1)}, f32[1,32,32]{2,1,0:T(8,128)S(1)}, u32[]{:S(2)}, u32[]{:S(2)}) collective-permute-start(f32[1,32,32]{2,1,0:T(8,128)S(1)} %get-tuple-element.315), channel_id=1, source_target_pairs={{0,32},{32,64},{64,96},{96,128},{128,160},{160,192},{192,224},{224... | collective-permute-start | bytes 12296 | tf_op jit(solution)/shard_map/while/body/eval_jaxpr/ppermute | solution.py:29
  286.2 11.6 %collective-permute-start = (f32[1,32,32]{2,1,0:T(8,128)S(1)}, f32[1,32,32]{2,1,0:T(8,128)S(1)}, u32[]{:S(2)}, u32[]{:S(2)}) collective-permute-start(f32[1,32,32]{2,1,0:T(8,128)S(1)} %get-tuple-element.315), channel_id=1, source_target_pairs={{0,32},{32,64},{64,96},{96,128},{128,160},{160,192},{192,224},{224... | collective-permute-start | bytes 12296 | tf_op jit(solution)/shard_map/while/body/eval_jaxpr/ppermute | solution.py:29
  307.7 11.6 %collective-permute-start = (f32[1,32,32]{2,1,0:T(8,128)S(1)}, f32[1,32,32]{2,1,0:T(8,128)S(1)}, u32[]{:S(2)}, u32[]{:S(2)}) collective-permute-start(f32[1,32,32]{2,1,0:T(8,128)S(1)} %get-tuple-element.315), channel_id=1, source_target_pairs={{0,32},{32,64},{64,96},{96,128},{128,160},{160,192},{192,224},{224... | collective-permute-start | bytes 12296 | tf_op jit(solution)/shard_map/while/body/eval_jaxpr/ppermute | solution.py:29
  329.2 11.6 %collective-permute-start = (f32[1,32,32]{2,1,0:T(8,128)S(1)}, f32[1,32,32]{2,1,0:T(8,128)S(1)}, u32[]{:S(2)}, u32[]{:S(2)}) collective-permute-start(f32[1,32,32]{2,1,0:T(8,128)S(1)} %get-tuple-element.315), channel_id=1, source_target_pairs={{0,32},{32,64},{64,96},{96,128},{128,160},{160,192},{192,224},{224... | collective-permute-start | bytes 12296 | tf_op jit(solution)/shard_map/while/body/eval_jaxpr/ppermute | solution.py:29
  350.7 11.6 %collective-permute-start = (f32[1,32,32]{2,1,0:T(8,128)S(1)}, f32[1,32,32]{2,1,0:T(8,128)S(1)}, u32[]{:S(2)}, u32[]{:S(2)}) collective-permute-start(f32[1,32,32]{2,1,0:T(8,128)S(1)} %get-tuple-element.315), channel_id=1, source_target_pairs={{0,32},{32,64},{64,96},{96,128},{128,160},{160,192},{192,224},{224... | collective-permute-start | bytes 12296 | tf_op jit(solution)/shard_map/while/body/eval_jaxpr/ppermute | solution.py:29
  372.2 11.6 %collective-permute-start = (f32[1,32,32]{2,1,0:T(8,128)S(1)}, f32[1,32,32]{2,1,0:T(8,128)S(1)}, u32[]{:S(2)}, u32[]{:S(2)}) collective-permute-start(f32[1,32,32]{2,1,0:T(8,128)S(1)} %get-tuple-element.315), channel_id=1, source_target_pairs={{0,32},{32,64},{64,96},{96,128},{128,160},{160,192},{192,224},{224... | collective-permute-start | bytes 12296 | tf_op jit(solution)/shard_map/while/body/eval_jaxpr/ppermute | solution.py:29
  393.7 11.6 %collective-permute-start = (f32[1,32,32]{2,1,0:T(8,128)S(1)}, f32[1,32,32]{2,1,0:T(8,128)S(1)}, u32[]{:S(2)}, u32[]{:S(2)}) collective-permute-start(f32[1,32,32]{2,1,0:T(8,128)S(1)} %get-tuple-element.315), channel_id=1, source_target_pairs={{0,32},{32,64},{64,96},{96,128},{128,160},{160,192},{192,224},{224... | collective-permute-start | bytes 12296 | tf_op jit(solution)/shard_map/while/body/eval_jaxpr/ppermute | solution.py:29
  415.3 11.6 %collective-permute-start = (f32[1,32,32]{2,1,0:T(8,128)S(1)}, f32[1,32,32]{2,1,0:T(8,128)S(1)}, u32[]{:S(2)}, u32[]{:S(2)}) collective-permute-start(f32[1,32,32]{2,1,0:T(8,128)S(1)} %get-tuple-element.315), channel_id=1, source_target_pairs={{0,32},{32,64},{64,96},{96,128},{128,160},{160,192},{192,224},{224... | collective-permute-start | bytes 12296 | tf_op jit(solution)/shard_map/while/body/eval_jaxpr/ppermute | solution.py:29
  436.8 11.6 %collective-permute-start = (f32[1,32,32]{2,1,0:T(8,128)S(1)}, f32[1,32,32]{2,1,0:T(8,128)S(1)}, u32[]{:S(2)}, u32[]{:S(2)}) collective-permute-start(f32[1,32,32]{2,1,0:T(8,128)S(1)} %get-tuple-element.315), channel_id=1, source_target_pairs={{0,32},{32,64},{64,96},{96,128},{128,160},{160,192},{192,224},{224... | collective-permute-start | bytes 12296 | tf_op jit(solution)/shard_map/while/body/eval_jaxpr/ppermute | solution.py:29
  458.3 11.6 %collective-permute-start = (f32[1,32,32]{2,1,0:T(8,128)S(1)}, f32[1,32,32]{2,1,0:T(8,128)S(1)}, u32[]{:S(2)}, u32[]{:S(2)}) collective-permute-start(f32[1,32,32]{2,1,0:T(8,128)S(1)} %get-tuple-element.315), channel_id=1, source_target_pairs={{0,32},{32,64},{64,96},{96,128},{128,160},{160,192},{192,224},{224... | collective-permute-start | bytes 12296 | tf_op jit(solution)/shard_map/while/body/eval_jaxpr/ppermute | solution.py:29
  479.8 11.6 %collective-permute-start = (f32[1,32,32]{2,1,0:T(8,128)S(1)}, f32[1,32,32]{2,1,0:T(8,128)S(1)}, u32[]{:S(2)}, u32[]{:S(2)}) collective-permute-start(f32[1,32,32]{2,1,0:T(8,128)S(1)} %get-tuple-element.315), channel_id=1, source_target_pairs={{0,32},{32,64},{64,96},{96,128},{128,160},{160,192},{192,224},{224... | collective-permute-start | bytes 12296 | tf_op jit(solution)/shard_map/while/body/eval_jaxpr/ppermute | solution.py:29
  (66 other events, 622.8 us)
where the time goes:
time: 505 us; the launch traced here: 503 us
  waiting for transfers between devices  260 us (51%)
  starting transfers between devices  141 us (28%)
  other arithmetic  57.1 us (11%)
  local copies, waits for them, and re-layouts  42.8 us (8%)
    ppermute x17, waiting for transfers between devices, passed_along(): return lax.ppermute(block, axis, route)  169 us
    ppermute x22, waiting for transfers between devices, with_halo(): lax.ppermute(lax.slice_in_dim(block, block.shape[dim] - width, None, axis...  91.4 us
    ppermute x22, starting transfers between devices, with_halo(): lax.ppermute(lax.slice_in_dim(block, 0, width, axis=dim), axis, backward)  55.3 us
    ppermute x22, starting transfers between devices, with_halo(): lax.ppermute(lax.slice_in_dim(block, block.shape[dim] - width, None, axis...  51.2 us
    ppermute x17, starting transfers between devices, passed_along(): return lax.ppermute(block, axis, route)  34.8 us
    reshape x1, local copies, waits for them, and re-layouts, down(): field.reshape(depth // 4, 4, width // 4, 4, height // 4, 4)  28.2 us
    reduce_sum x8, other arithmetic, down(): field.reshape(depth // 4, 4, width // 4, 4, height // 4, 4)  16.9 us
    mul x3, other arithmetic, on_device(): fine_field = stepped * inside[lower + 1:lower + length - 1][:, None, None]  15.2 us
  transfers between devices with their start and end apart: 61, of which 36 were waited for; matrix products, arithmetic and copies ran while one was open for 3% of the time, Pallas kernels for 0%

commit v1 on v0

v1 whole, which is shorter than its diff:
```python
import functools

import jax
import jax.numpy as jnp
from jax import lax
from jax.experimental import pallas as pl
from jax.experimental.pallas import tpu as pltpu
from jax.sharding import PartitionSpec as P

FSTEPS = 4
CSTEPS = 1
STEP = 0.06
MESH = pl.DeviceIdType.MESH
F32 = jnp.float32
NG = 32
NT = 16


def dot(a, b):
    return jnp.dot(a, b, precision=lax.Precision.HIGHEST, preferred_element_type=F32)


def iota(shape, dim):
    return lax.broadcasted_iota(jnp.int32, shape, dim)


def ones_where(mask):
    return jnp.where(mask, F32(1.0), F32(0.0))


def pool_mats():
    cols = ones_where(iota((128, 128), 0) // 4 == iota((128, 128), 1) % 32)
    rows = ones_where(iota((32, 128), 0) == iota((32, 128), 1) // 4)
    return cols, rows


def pool(total, mats):
    cols, rows = mats
    u = dot(rows, dot(total, cols))
    group = iota((8, 128), 1) // 32
    out = jnp.zeros((8, 128), F32)
    for g in range(4):
        out = out + jnp.where(group == g, u[8 * g : 8 * g + 8], F32(0.0))
    return out * F32(1.0 / 64.0)


def unpool(coarse):
    group = iota((8, 128), 1) // 32
    u = jnp.concatenate([jnp.where(group == g, coarse, F32(0.0)) for g in range(4)], axis=0)
    rows_t = ones_where(iota((128, 32), 0) // 4 == iota((128, 32), 1))
    cols_t = ones_where(iota((128, 128), 0) % 32 == iota((128, 128), 1) // 4)
    return dot(dot(rows_t, u), cols_t)


def release(v, hp, act):
    return hp * jnp.exp(act * v / (1.0 + jnp.abs(v)))


def lookup(ids, table):
    return jnp.where(ids == 0, table[0], jnp.where(ids == 1, table[1], table[2]))


def coarse_shifts(v):
    row = iota(v.shape, 1)
    right = pltpu.roll(v, 127, 2)
    left = pltpu.roll(v, 1, 2)
    up = pltpu.roll(v, 7, 1)
    up = jnp.where(row == 7, pltpu.roll(up, 96, 2), up)
    down = pltpu.roll(v, 1, 1)
    down = jnp.where(row == 0, pltpu.roll(down, 32, 2), down)
    return right, left, up, down


def coarse_coefs(k, p, outside, inside):
    scale = F32(STEP * FSTEPS / CSTEPS / 16.0 * 0.5)
    n = k.shape[0] - 2
    mid = k[1:-1]
    lane = iota(mid.shape, 2)
    row = iota(mid.shape, 1)
    right, left, up, down = coarse_shifts(mid)
    edges = (
        (right, lane % 32 == 31),
        (left, lane % 32 == 0),
        (up, (row == 7) & (lane >= 96)),
        (down, (row == 0) & (lane < 32)),
    )
    keep = F32(1.0)
    sides = []
    for other, edge in edges:
        face = scale * (mid + jnp.where(edge, outside, other))
        keep = keep - face
        sides.append(jnp.where(edge, F32(0.0), face))
    faces = scale * (k[1:] + k[:-1])
    keep = keep - faces[1:] - faces[:-1]
    both = [jnp.where(inside[i] & inside[i + 1], faces[i : i + 1], F32(0.0)) for i in range(n + 1)]
    vertical = jnp.concatenate(both, axis=0)
    return sides, vertical, keep, F32(STEP * FSTEPS / CSTEPS) * p


def coarse_step(c, sides, below, above, keep, hp, act):
    mid = c[1:-1]
    out = mid * keep + below * c[:-2] + above * c[2:]
    for other, face in zip(coarse_shifts(mid), sides):
        out = out + face * other
    return out + release(mid, hp, act)


def kernel(
    starts,
    materials,
    cond,
    pre,
    act,
    out,
    fa,
    fb,
    ids,
    kbuf,
    kz,
    kxr,
    kxl,
    kyu,
    kyd,
    keep,
    hp,
    actb,
    fprev,
    oldv,
    gbuf,
    dbuf,
    c8,
    gs,
    cz,
    cside,
    ckeep,
    chp,
    local_sem,
    slab_s,
    slab_r,
    c0_s,
    c0_r,
    gc_s,
    gc_r,
    dt_s,
    dt_r,
    dg_s,
    dg_r,
    cr_s,
    cr_r,
    f_s,
    f_r,
    know,
):
    tm = lax.axis_index("tm")
    gz = lax.axis_index("gz")
    zi = lax.rem(tm, 8)
    hi = tm // 8
    yy = hi * 4 + gz // 8
    rest = lax.rem(gz, 8)

    def ring(k):
        return (hi * 8 + lax.rem(zi + (k % 8), 8), gz)

    def ygo(k):
        y = lax.rem(yy + (k % 8), 8)
        return ((y // 4) * 8 + zi, lax.rem(y, 4) * 8 + rest)

    def has(j):
        return (gz + j >= 0) & (gz + j < NG)

    def remote(src, dst, send, recv, where):
        return pltpu.make_async_remote_copy(
            src_ref=src, dst_ref=dst, send_sem=send, recv_sem=recv, device_id=where, device_id_type=MESH
        )

    def tell(sem, where):
        pl.semaphore_signal(sem, 1, device_id=where, device_id_type=MESH)

    def tell_layers(sem, dist):
        for j in (-dist, dist):

            @pl.when(has(j))
            def _():
                tell(sem, (tm, gz + j))

    def hear(sem, dist, more):
        pl.semaphore_wait(sem, has(-dist).astype(jnp.int32) + has(dist).astype(jnp.int32) + more)

    c0, is_b = cond[0], hi == 1

    own_f = pltpu.make_async_copy(starts, fa.at[pl.ds(4, 4)], local_sem.at[0])
    own_m = pltpu.make_async_copy(materials, ids.at[pl.ds(4, 4)], local_sem.at[1])
    own_m.start()
    own_f.start()
    for j, at in ((-1, 0), (1, 8)):

        @pl.when(jnp.logical_not(has(j)))
        def _():
            fa[pl.ds(at, 4)] = jnp.zeros((4, 128, 128), F32)
            ids[pl.ds(at, 4)] = jnp.zeros((4, 128, 128), jnp.int32)

    gbuf[...] = jnp.zeros(gbuf.shape, F32)
    gbuf[:, 0] = jnp.full((17, 8, 128), c0, F32)
    dbuf[...] = jnp.zeros(dbuf.shape, F32)
    c8[...] = jnp.zeros(c8.shape, F32)

    barrier = pltpu.get_barrier_semaphore()
    tell_layers(barrier, 1)
    for k in (1, -1):
        tell(barrier, ring(k))
        tell(barrier, ygo(k))
    hear(barrier, 1, 4)

    def slab(j, n, what):
        side = 0 if j > 0 else 1
        here = 3 - n if j > 0 else n
        there = here if j > 0 else 8 + here
        src, dst = (starts, fa) if what == 0 else (materials, ids)
        return remote(
            src.at[here], dst.at[there], slab_s.at[side, n, what], slab_r.at[side, n, what], (tm, gz + j)
        )

    for n in range(4):
        for j in (1, -1):

            @pl.when(has(j))
            def _():
                slab(j, n, 1).start()
                slab(j, n, 0).start()

    tell_layers(know.at[0], 1)
    for k in (1, -1):
        tell(know.at[0], ring(k))
        tell(know.at[0], ygo(k))

    mats = pool_mats()
    own_m.wait()
    totals = [jnp.zeros((128, 128), F32) for _ in range(3)]
    for n in range(4):
        layer = ids[4 + n]
        totals = [t + lookup(layer, table) for t, table in zip(totals, (cond, pre, act))]
    for i in range(3):
        gbuf[8, i] = pool(totals[i], mats)
    own_f.wait()
    own_coarse = pool(fa[4] + fa[5] + fa[6] + fa[7], mats)

    @pl.when((tm == 0) | is_b)
    def _():
        gbuf[8, 3] = jnp.where(is_b, F32(0.0), own_coarse)

    out[...] = fa[pl.ds(4, 4)]

    hear(know.at[0], 1, 4)
    tell_layers(know.at[1], 2)
    for k in (2, -2):
        tell(know.at[1], ring(k))
        tell(know.at[1], ygo(k))
    hear(know.at[1], 2, 4)
    tell_layers(know.at[2], 4)
    tell(know.at[2], ygo(4))

    def c0_copy(n):
        return remote(gbuf.at[8, 3], gbuf.at[8, 3], c0_s.at[n - 1], c0_r, (n, gz))

    @pl.when(tm == 0)
    def _():
        for n in range(1, 8):
            c0_copy(n).start()

    for n in range(4):
        for j in (1, -1):

            @pl.when(has(-j))
            def _():
                slab(j, n, 1).wait_recv()
                slab(j, n, 0).wait_recv()

    lane = iota((128, 128), 1)
    row = iota((128, 128), 0)

    def inside_fine(layer):
        return jnp.logical_not(((layer < 4) & (gz == 0)) | ((layer >= 8) & (gz == NG - 1)))

    def conduct(layer, _):
        kbuf[layer] = lookup(ids[layer], cond)
        return 0

    lax.fori_loop(0, 12, conduct, 0)
    half = F32(0.5 * STEP)

    def fine_coef(layer, _):
        k = kbuf[layer]
        inside = inside_fine(layer)
        above = half * (k + kbuf[layer + 1])
        below = half * (k + kbuf[layer - 1])
        rest_of = 1.0 - above - below
        for other, edge, ref in (
            (pltpu.roll(k, 127, 1), lane == 127, kxr),
            (pltpu.roll(k, 1, 1), lane == 0, kxl),
            (pltpu.roll(k, 127, 0), row == 127, kyu),
            (pltpu.roll(k, 1, 0), row == 0, kyd),
        ):
            face = half * (k + jnp.where(edge, c0, other))
            rest_of = rest_of - face
            ref[layer] = jnp.where(edge, F32(0.0), face)
        keep[layer] = rest_of
        kz[layer] = jnp.where(inside & inside_fine(layer + 1), above, F32(0.0))

        @pl.when(layer == 1)
        def _():
            kz[0] = jnp.where(inside & inside_fine(layer - 1), below, F32(0.0))

        ident = ids[layer]
        hp[layer] = jnp.where(inside, F32(STEP) * lookup(ident, pre), F32(0.0))
        actb[layer] = lookup(ident, act)
        return 0

    lax.fori_loop(1, 11, fine_coef, 0)

    k_near = jnp.stack(
        [
            pool(kbuf[0] + kbuf[1] + kbuf[2] + kbuf[3], mats),
            gbuf[8, 0],
            pool(kbuf[8] + kbuf[9] + kbuf[10] + kbuf[11], mats),
        ]
    )
    near = jnp.stack(
        [
            pool(fa[0] + fa[1] + fa[2] + fa[3], mats),
            own_coarse,
            pool(fa[8] + fa[9] + fa[10] + fa[11], mats),
        ]
    )
    sides, vertical, kept, heat = coarse_coefs(k_near, gbuf[8, 1][None], c0, [has(-1), has(0), has(1)])
    old = coarse_step(near, sides, vertical[:1], vertical[1:], kept, heat, gbuf[8, 2][None])[0]
    oldv[0] = old

    for step in range(FSTEPS):
        src, dst = (fa, fb) if step % 2 == 0 else (fb, fa)

        def fine_step(layer, _):
            v = src[layer]
            new = v * keep[layer] + kz[layer - 1] * src[layer - 1] + kz[layer] * src[layer + 1]
            new = new + kxr[layer] * pltpu.roll(v, 127, 1) + kxl[layer] * pltpu.roll(v, 1, 1)
            new = new + kyu[layer] * pltpu.roll(v, 127, 0) + kyd[layer] * pltpu.roll(v, 1, 0)
            dst[layer] = new + release(v, hp[layer], actb[layer])
            return 0

        lax.fori_loop(step + 1, 11 - step, fine_step, 0)
    d_own = pool(fa[4] + fa[5] + fa[6] + fa[7], mats) - old
    dbuf[7, zi] = d_own

    def dt_copy(k):
        return remote(dbuf.at[7, zi], dbuf.at[7, zi], dt_s.at[k - 1], dt_r.at[k - 1], ring(k))

    for k in range(1, 8):
        dt_copy(k).start()

    hear(know.at[2], 4, 1)
    tell(know.at[3], ygo(4))

    def pass_fine():
        return remote(fa.at[pl.ds(4, 4)], fprev, f_s.at[0], f_r.at[0], (tm + 1, gz))

    def pass_old():
        return remote(oldv.at[0], oldv.at[1], f_s.at[1], f_r.at[1], (tm + 1, gz))

    @pl.when(tm < NT - 1)
    def _():
        pass_old().start()
        pass_fine().start()

    @pl.when((tm > 0) & (tm < 8))
    def _():
        c0_copy(1).wait_recv()

    def gc_copy(j):
        i = j + 8 if j < 0 else j + 7
        return remote(gbuf.at[8], gbuf.at[8 - j], gc_s.at[i], gc_r.at[i], (tm, gz + j))

    around = [j for d in range(1, 9) for j in (d, -d)]
    for j in around:

        @pl.when(has(j))
        def _():
            gc_copy(j).start()

    for k in range(1, 8):
        dt_copy(k).wait_recv()

    def dg_copy(j):
        i = j + 7 if j < 0 else j + 6
        n = 8 - abs(j)
        return remote(
            dbuf.at[7, pl.ds(0, n)], dbuf.at[7 - j, pl.ds(0, n)], dg_s.at[i], dg_r.at[i], (tm, gz + j)
        )

    for j in around[:14]:

        @pl.when(has(j))
        def _():
            dg_copy(j).start()

    for j in around:

        @pl.when(has(-j))
        def _():
            gc_copy(j).wait_recv()

    sides, vertical, kept, heat = coarse_coefs(gbuf[:, 0], gbuf[1:16, 1], c0, [has(j) for j in range(-8, 9)])
    for i in range(4):
        cside[i] = sides[i]
    cz[...] = vertical
    ckeep[...] = kept
    chp[...] = heat

    for j in around[:14]:

        @pl.when(has(-j))
        def _():
            dg_copy(j).wait_recv()

    def cr_copy(j):
        return remote(gs.at[9], c8.at[8 - j], cr_s.at[j + 7], cr_r.at[j + 7], (tm + 8, gz + j))

    def g8_copy():
        return remote(gs.at[8], gs.at[0], cr_s.at[15], cr_r.at[15], (tm + 8, gz))

    for j in range(-7, 8):

        @pl.when(is_b & has(-j) & (zi >= abs(j)))
        def _():
            cr_copy(j).wait_recv()

    @pl.when(is_b)
    def _():
        g8_copy().wait_recv()

    state = jnp.where(is_b, c8[...], gbuf[:, 3])
    for s in range(1, 9):
        n = 17 - 2 * s
        lo = s - 1
        latest = coarse_step(
            state,
            [cside[i, pl.ds(lo, n)] for i in range(4)],
            cz[pl.ds(lo, n)],
            cz[pl.ds(lo + 1, n)],
            ckeep[pl.ds(lo, n)],
            chp[pl.ds(lo, n)],
            gbuf[pl.ds(lo + 1, n), 2],
        )
        gs[s] = latest[8 - s]
        state = latest + dbuf[pl.ds(lo, n), s - 1]
    gs[9] = state[0]

    is_a = jnp.logical_not(is_b)
    pl.semaphore_wait(know.at[3], 1)
    for j in range(-7, 8):

        @pl.when(is_a & has(j) & (zi >= abs(j)))
        def _():
            cr_copy(j).start()

    @pl.when(is_a)
    def _():
        g8_copy().start()

    @pl.when(tm > 0)
    def _():
        pass_old().wait_recv()
        pass_fine().wait_recv()
        fine = unpool(gs[zi] - oldv[1])
        for n in range(4):
            out[n] = fprev[n] + fine

    for n in range(4):
        for j in (1, -1):

            @pl.when(has(j))
            def _():
                slab(j, n, 1).wait_send()
                slab(j, n, 0).wait_send()

    @pl.when(tm == 0)
    def _():
        for n in range(1, 8):
            c0_copy(n).wait_send()

    for k in range(1, 8):
        dt_copy(k).wait_send()

    @pl.when(tm < NT - 1)
    def _():
        pass_old().wait_send()
        pass_fine().wait_send()

    for j in around:

        @pl.when(has(j))
        def _():
            gc_copy(j).wait_send()

    for j in around[:14]:

        @pl.when(has(j))
        def _():
            dg_copy(j).wait_send()

    for j in range(-7, 8):

        @pl.when(is_a & has(j) & (zi >= abs(j)))
        def _():
            cr_copy(j).wait_send()

    @pl.when(is_a)
    def _():
        g8_copy().wait_send()


def on_device(starts, materials, conductivity, pre_factor, activation):
    vmem, dma = pltpu.VMEM, pltpu.SemaphoreType.DMA
    slabs = vmem((12, 128, 128), F32)
    tile = lambda *lead: vmem(lead + (8, 128), F32)
    result = pl.pallas_call(
        kernel,
        name="parareal",
        out_shape=jax.ShapeDtypeStruct((4, 128, 128), F32),
        in_specs=[pl.BlockSpec(memory_space=pl.ANY)] * 2 + [pl.BlockSpec(memory_space=pltpu.SMEM)] * 3,
        out_specs=pl.BlockSpec(memory_space=pltpu.VMEM),
        scratch_shapes=[
            slabs,
            slabs,
            vmem((12, 128, 128), jnp.int32),
            *([slabs] * 9),
            vmem((4, 128, 128), F32),
            tile(2),
            tile(17, 4),
            tile(15, 8),
            tile(17),
            tile(10),
            tile(16),
            tile(4, 15),
            tile(15),
            tile(15),
            dma((2,)),
            dma((2, 4, 2)),
            dma((2, 4, 2)),
            dma((7,)),
            dma(()),
            dma((16,)),
            dma((16,)),
            dma((7,)),
            dma((7,)),
            dma((14,)),
            dma((14,)),
            dma((16,)),
            dma((16,)),
            dma((2,)),
            dma((2,)),
            pltpu.SemaphoreType.REGULAR((4,)),
        ],
        compiler_params=pltpu.CompilerParams(
            collective_id=0, has_side_effects=True, vmem_limit_bytes=40 * 2**20
        ),
        cost_estimate=pl.CostEstimate(flops=50_000_000, bytes_accessed=2_000_000, transcendentals=500_000),
    )(starts[0], materials, conductivity, pre_factor, activation)
    return result[None]


def solution(mesh):
    return jax.shard_map(
        on_device,
        mesh=mesh,
        in_specs=(P("tm", "gz", None, None), P("gz", None, None), P(), P(), P()),
        out_specs=P("tm", "gz", None, None),
        check_vma=False,
    )
```

time: 505 us -> 49.3 us (0.10)
  the two profiles are of different devices: /device:TPU:56 before, /device:TPU:505 now
where the time goes in v1:
time: 49.3 us; the launch traced here: 49.1 us
  Pallas kernels  45.8 us (93%)
  local copies, waits for them, and re-layouts  3.29 us (7%)
    pallas_call x1, Pallas kernels, on_device(): pl.pallas_call(kernel, name='parareal', out_shape=jax.ShapeDtypeStruct((4...  45.8 us
    unnamed x11, local copies, waits for them, and re-layouts  3.29 us

profile of v1, /device:TPU:505, one launch (start us, length us, event | category | flops | bytes accessed | tf_op | source)
XLA Modules:
  0.0 49.1 jit_solution(4731216011954439018)
XLA Ops:
  0.0 0.0 copy-start.4
  0.0 0.0 copy-start.3
  0.0 0.0 copy-start.2
  0.0 0.6 %copy-done.4 = f32[3]{0:T(128)S(1)} copy-done((f32[3]{0:T(128)S(1)}, f32[3]{0:T(128)}, u32[]{:S(2)}) %copy-start.4) | copy-done | bytes 36
  0.7 0.0 copy-done.3
  0.7 0.0 copy-done.2
  0.7 0.0 copy-start
  0.7 0.9 %copy-done = f32[1,4,128,128]{3,2,1,0:T(8,128)S(1)} copy-done((f32[1,4,128,128]{3,2,1,0:T(8,128)S(1)}, f32[1,4,128,128]{3,2,1,0:T(8,128)}, u32[]{:S(2)}) %copy-start) | copy-done | bytes 262168
  1.6 0.0 copy-start.1
  1.6 0.9 %copy-done.1 = s32[4,128,128]{2,1,0:T(8,128)S(1)} copy-done((s32[4,128,128]{2,1,0:T(8,128)S(1)}, s32[4,128,128]{2,1,0:T(8,128)}, u32[]{:S(2)}) %copy-start.1) | copy-done | bytes 262168
  2.6 45.8 %parareal.1 = f32[4,128,128]{2,1,0:T(8,128)S(1)} custom-call(f32[4,128,128]{2,1,0:T(8,128)S(1)} %bitcast.3, s32[4,128,128]{2,1,0:T(8,128)S(1)} %copy-done.1, f32[3]{0:T(128)S(1)} %copy-done.2, f32[3]{0:T(128)S(1)} %copy-done.3, f32[3]{0:T(128)S(1)} %copy-done.4), custom_call_target="tpu_custom_call" | custom-call | flops 50000000 | bytes 2000000 | tf_op jit(solution)/shard_map/parareal/pallas_call | solution.py:524
  48.4 0.7 %copy.7 = f32[1,4,128,128]{3,2,1,0:T(8,128)} copy(f32[1,4,128,128]{3,2,1,0:T(8,128)S(1)} %bitcast.2) | data formatting | bytes 524288
Async XLA Ops:
  0.0 0.7 %copy-start.4 = (f32[3]{0:T(128)S(1)}, f32[3]{0:T(128)}, u32[]{:S(2)}) copy-start(f32[3]{0:T(128)} %act.1) | copy-start | bytes 40
  0.0 0.7 %copy-start.3 = (f32[3]{0:T(128)S(1)}, f32[3]{0:T(128)}, u32[]{:S(2)}) copy-start(f32[3]{0:T(128)} %pre.1) | copy-start | bytes 40
  0.0 0.7 %copy-start.2 = (f32[3]{0:T(128)S(1)}, f32[3]{0:T(128)}, u32[]{:S(2)}) copy-start(f32[3]{0:T(128)} %cond.1) | copy-start | bytes 40
  0.7 0.9 %copy-start = (f32[1,4,128,128]{3,2,1,0:T(8,128)S(1)}, f32[1,4,128,128]{3,2,1,0:T(8,128)}, u32[]{:S(2)}) copy-start(f32[1,4,128,128]{3,2,1,0:T(8,128)} %param.5) | copy-start | bytes 786436
  1.6 0.9 %copy-start.1 = (s32[4,128,128]{2,1,0:T(8,128)S(1)}, s32[4,128,128]{2,1,0:T(8,128)}, u32[]{:S(2)}) copy-start(s32[4,128,128]{2,1,0:T(8,128)} %materials.1) | copy-start | bytes 786436

commit v2 on v1

v2 whole, which is shorter than its diff:
```python
import functools

import jax
import jax.numpy as jnp
from jax import lax
from jax.experimental import pallas as pl
from jax.experimental.pallas import tpu as pltpu
from jax.sharding import PartitionSpec as P

FSTEPS = 4
CSTEPS = 1
STEP = 0.06
MESH = pl.DeviceIdType.MESH
F32 = jnp.float32
NG = 32
NT = 16


def dot(a, b):
    return jnp.dot(a, b, precision=lax.Precision.HIGHEST, preferred_element_type=F32)


def iota(shape, dim):
    return lax.broadcasted_iota(jnp.int32, shape, dim)


def ones_where(mask):
    return jnp.where(mask, F32(1.0), F32(0.0))


def pool(totals):
    n = len(totals)
    cols = ones_where(iota((128, 128), 0) // 4 == iota((128, 128), 1) % 32)
    rows = ones_where(iota((32, 128), 0) == iota((32, 128), 1) // 4)
    wide = dot(rows, jnp.concatenate(totals, axis=1))
    tall = dot(jnp.concatenate([wide[:, 128 * i : 128 * i + 128] for i in range(n)], axis=0), cols)
    group = iota((8, 128), 1) // 32
    outs = []
    for i in range(n):
        out = jnp.zeros((8, 128), F32)
        for g in range(4):
            at = 32 * i + 8 * g
            out = out + jnp.where(group == g, tall[at : at + 8], F32(0.0))
        outs.append(out * F32(1.0 / 64.0))
    return outs


def unpool(coarse):
    group = iota((8, 128), 1) // 32
    u = jnp.concatenate([jnp.where(group == g, coarse, F32(0.0)) for g in range(4)], axis=0)
    rows_t = ones_where(iota((128, 32), 0) // 4 == iota((128, 32), 1))
    cols_t = ones_where(iota((128, 128), 0) % 32 == iota((128, 128), 1) // 4)
    return dot(rows_t, dot(u, cols_t))


def release(v, hp, act):
    return hp * jnp.exp(act * v / (1.0 + jnp.abs(v)))


def lookup(ids, table):
    return jnp.where(ids == 0, table[0], jnp.where(ids == 1, table[1], table[2]))


def coarse_shifts(v):
    row = iota(v.shape, 1)
    right = pltpu.roll(v, 127, 2)
    left = pltpu.roll(v, 1, 2)
    up = pltpu.roll(v, 7, 1)
    up = jnp.where(row == 7, pltpu.roll(up, 96, 2), up)
    down = pltpu.roll(v, 1, 1)
    down = jnp.where(row == 0, pltpu.roll(down, 32, 2), down)
    return right, left, up, down


def coarse_coefs(k, p, outside, inside):
    scale = F32(STEP * FSTEPS / CSTEPS / 16.0 * 0.5)
    n = k.shape[0] - 2
    mid = k[1:-1]
    lane = iota(mid.shape, 2)
    row = iota(mid.shape, 1)
    right, left, up, down = coarse_shifts(mid)
    edges = (
        (right, lane % 32 == 31),
        (left, lane % 32 == 0),
        (up, (row == 7) & (lane >= 96)),
        (down, (row == 0) & (lane < 32)),
    )
    keep = F32(1.0)
    sides = []
    for other, edge in edges:
        face = scale * (mid + jnp.where(edge, outside, other))
        keep = keep - face
        sides.append(jnp.where(edge, F32(0.0), face))
    faces = scale * (k[1:] + k[:-1])
    keep = keep - faces[1:] - faces[:-1]
    both = [jnp.where(inside[i] & inside[i + 1], faces[i : i + 1], F32(0.0)) for i in range(n + 1)]
    vertical = jnp.concatenate(both, axis=0)
    return sides, vertical, keep, F32(STEP * FSTEPS / CSTEPS) * p


def coarse_step(c, sides, below, above, keep, hp, act):
    mid = c[1:-1]
    out = mid * keep + below * c[:-2] + above * c[2:]
    for other, face in zip(coarse_shifts(mid), sides):
        out = out + face * other
    return out + release(mid, hp, act)


def kernel(
    starts,
    materials,
    cond,
    pre,
    act,
    out,
    fab,
    ids,
    kbuf,
    kz,
    kxr,
    kxl,
    kyu,
    kyd,
    keep,
    hp,
    actb,
    fprev,
    relay,
    oldv,
    near,
    gbuf,
    dbuf,
    c8,
    state,
    gs,
    cz,
    cside,
    ckeep,
    chp,
    local_sem,
    near_s,
    near_r,
    slab_s,
    slab_r,
    c0_s,
    c0_r,
    gc_s,
    gc_r,
    dt_s,
    dt_r,
    dg_s,
    dg_r,
    dl_s,
    dl_r,
    cr_s,
    cr_r,
    f_s,
    f_r,
    rl_s,
    rl_r,
    know,
):
    tm = lax.axis_index("tm")
    gz = lax.axis_index("gz")
    zi = lax.rem(tm, 8)
    hi = tm // 8
    yy = hi * 4 + gz // 8
    rest = lax.rem(gz, 8)

    def ring(k):
        return (hi * 8 + lax.rem(zi + (k % 8), 8), gz)

    def ygo(k):
        y = lax.rem(yy + (k % 8), 8)
        return ((y // 4) * 8 + zi, lax.rem(y, 4) * 8 + rest)

    def has(j):
        return (gz + j >= 0) & (gz + j < NG)

    def has_slice(k):
        return (zi + k >= 0) & (zi + k < 8)

    def remote(src, dst, send, recv, where):
        return pltpu.make_async_remote_copy(
            src_ref=src, dst_ref=dst, send_sem=send, recv_sem=recv, device_id=where, device_id_type=MESH
        )

    pending = []

    def send(when, *copies):
        @pl.when(when)
        def _():
            for copy in copies:
                copy().start()

        pending.append((when, copies))

    def finish():
        for when, copies in pending:

            @pl.when(when)
            def _(copies=copies):
                for copy in copies:
                    copy().wait_send()

    def tell_one(sem, where):
        pl.semaphore_signal(sem, 1, device_id=where, device_id_type=MESH)

    def tell(sem, dist):
        for j in (-dist, dist):

            @pl.when(has(j))
            def _():
                tell_one(sem, (tm, gz + j))

            @pl.when(has_slice(j))
            def _():
                tell_one(sem, (tm + j, gz))

        tell_one(sem, ygo(dist))
        if dist < 4:
            tell_one(sem, ygo(-dist))

    def hear(sem, dist):
        n = 1 if dist == 4 else 2
        for j in (-dist, dist):
            n = n + has(j).astype(jnp.int32) + has_slice(j).astype(jnp.int32)
        pl.semaphore_wait(sem, n)

    c0, is_b = cond[0], hi == 1
    is_a = jnp.logical_not(is_b)

    own_f = pltpu.make_async_copy(starts, fab.at[0, pl.ds(4, 4)], local_sem.at[0])
    own_m = pltpu.make_async_copy(materials, ids.at[pl.ds(4, 4)], local_sem.at[1])
    own_m.start()
    own_f.start()
    for j, at in ((-1, 0), (1, 8)):

        @pl.when(jnp.logical_not(has(j)))
        def _():
            fab[0, pl.ds(at, 4)] = jnp.zeros((4, 128, 128), F32)
            ids[pl.ds(at, 4)] = jnp.zeros((4, 128, 128), jnp.int32)

    near[...] = jnp.zeros(near.shape, F32)
    gbuf[...] = jnp.zeros(gbuf.shape, F32)
    gbuf[:, 0] = jnp.full((17, 8, 128), c0, F32)
    dbuf[...] = jnp.zeros(dbuf.shape, F32)
    c8[...] = jnp.zeros(c8.shape, F32)

    barrier = pltpu.get_barrier_semaphore()
    tell(barrier, 1)

    own_m.wait()
    totals = [jnp.zeros((128, 128), F32) for _ in range(3)]
    for n in range(4):
        layer = ids[4 + n]
        totals = [t + lookup(layer, table) for t, table in zip(totals, (cond, pre, act))]
    own_f.wait()
    totals.append(fab[0, 4] + fab[0, 5] + fab[0, 6] + fab[0, 7])
    pooled = pool(totals)
    for i in range(3):
        gbuf[8, i] = pooled[i]
    own_coarse = pooled[3]
    near[1, 0] = pooled[0]
    near[1, 1] = own_coarse

    @pl.when(tm == 0)
    def _():
        dbuf[8, 0] = own_coarse
        out[...] = fab[0, pl.ds(4, 4)]

    hear(barrier, 1)

    def near_copy(j):
        side = 0 if j > 0 else 1
        return remote(near.at[1], near.at[1 - j], near_s.at[side], near_r.at[side], (tm, gz + j))

    def slab(j, n, what):
        side = 0 if j > 0 else 1
        here = 3 - n if j > 0 else n
        there = here if j > 0 else 8 + here
        src = (starts if what == 0 else materials).at[here]
        dst = fab.at[0, there] if what == 0 else ids.at[there]
        return remote(src, dst, slab_s.at[side, n, what], slab_r.at[side, n, what], (tm, gz + j))

    for j in (1, -1):
        send(has(j), functools.partial(near_copy, j))
    for n in range(4):
        for j in (1, -1):
            send(has(j), functools.partial(slab, j, n, 1), functools.partial(slab, j, n, 0))
    tell(know.at[0], 1)

    lane = iota((128, 128), 1)
    row = iota((128, 128), 0)
    half = F32(0.5 * STEP)

    def inside_fine(layer):
        return jnp.logical_not(((layer < 4) & (gz == 0)) | ((layer >= 8) & (gz == NG - 1)))

    def sources(layer):
        ident, inside = ids[layer], inside_fine(layer)
        kbuf[layer] = lookup(ident, cond)
        hp[layer] = jnp.where(inside, F32(STEP) * lookup(ident, pre), F32(0.0))
        actb[layer] = lookup(ident, act)

    def faces(layer):
        k = kbuf[layer]
        inside = inside_fine(layer)
        above = half * (k + kbuf[layer + 1])
        below = half * (k + kbuf[layer - 1])
        rest_of = 1.0 - above - below
        for other, edge, ref in (
            (pltpu.roll(k, 127, 1), lane == 127, kxr),
            (pltpu.roll(k, 1, 1), lane == 0, kxl),
            (pltpu.roll(k, 127, 0), row == 127, kyu),
            (pltpu.roll(k, 1, 0), row == 0, kyd),
        ):
            face = half * (k + jnp.where(edge, c0, other))
            rest_of = rest_of - face
            ref[layer] = jnp.where(edge, F32(0.0), face)
        keep[layer] = rest_of
        kz[layer] = jnp.where(inside & inside_fine(layer + 1), above, F32(0.0))
        kz[layer - 1] = jnp.where(inside & inside_fine(layer - 1), below, F32(0.0))

    def fine_step(layer, at):
        v = fab[at, layer]
        new = v * keep[layer] + kz[layer - 1] * fab[at, layer - 1] + kz[layer] * fab[at, layer + 1]
        new = new + kxr[layer] * pltpu.roll(v, 127, 1) + kxl[layer] * pltpu.roll(v, 1, 1)
        new = new + kyu[layer] * pltpu.roll(v, 127, 0) + kyd[layer] * pltpu.roll(v, 1, 0)
        fab[1 - at, layer] = new + release(v, hp[layer], actb[layer])

    def slab_here(n):
        for j in (1, -1):

            @pl.when(has(-j))
            def _():
                slab(j, n, 1).wait_recv()
                slab(j, n, 0).wait_recv()

    def stage(n):
        sources(3 - n)
        sources(8 + n)
        if n == 0:

            def own_faces(i, _):
                faces(4 + i)
                return 0

            lax.fori_loop(0, 4, own_faces, 0)
        else:
            faces(4 - n)
            faces(7 + n)

        def pair(i, _):
            at = lax.rem(jnp.minimum(i, n), 2)
            fine_step(4 - n + i, at)
            fine_step(7 + n - i, at)
            return 0

        lax.fori_loop(0, n + 2, pair, 0)

    def own_sources(i, _):
        sources(4 + i)
        return 0

    lax.fori_loop(0, 4, own_sources, 0)
    hear(know.at[0], 1)
    tell(know.at[1], 2)
    for j in (1, -1):

        @pl.when(has(-j))
        def _():
            near_copy(j).wait_recv()

    @pl.when(jnp.logical_not(has(-1)))
    def _():
        near[0, 0] = jnp.full((8, 128), c0, F32)

    @pl.when(jnp.logical_not(has(1)))
    def _():
        near[2, 0] = jnp.full((8, 128), c0, F32)

    sides, vertical, kept, heat = coarse_coefs(
        near[:, 0], gbuf[8, 1][None], c0, [has(-1), has(0), has(1)]
    )
    old = coarse_step(near[:, 1], sides, vertical[:1], vertical[1:], kept, heat, gbuf[8, 2][None])[0]
    oldv[0] = old

    hear(know.at[1], 2)
    tell(know.at[2], 4)
    for n in range(3):
        slab_here(n)
        stage(n)
    hear(know.at[2], 4)
    tell_one(know.at[3], ygo(4))
    tell_one(know.at[3], ring(1))
    tell_one(know.at[3], ring(-1))

    def c0_copy(n):
        return remote(dbuf.at[8, 0], dbuf.at[8, 0], c0_s.at[n - 1], c0_r, (n, gz))

    send(tm == 0, *[functools.partial(c0_copy, n) for n in range(1, 8)])
    slab_here(3)

    def gc_copy(j):
        i = j + 8 if j < 0 else j + 7
        return remote(gbuf.at[8], gbuf.at[8 - j], gc_s.at[i], gc_r.at[i], (tm, gz + j))

    around = [j for d in range(1, 9) for j in (d, -d)]
    for j in around:
        send(has(j), functools.partial(gc_copy, j))

    stage(3)
    dbuf[8, zi + 1] = pool([fab[0, 4] + fab[0, 5] + fab[0, 6] + fab[0, 7]])[0] - old

    def dt_copy(k):
        own = dbuf.at[8, zi + 1]
        return remote(own, own, dt_s.at[k - 1], dt_r.at[zi], ring(k))

    send(tm >= 0, *[functools.partial(dt_copy, k) for k in (4, 3, 5, 2, 6, 1, 7)])

    def dt_here(first, last):
        for at in range(first, last):

            @pl.when(zi != at)
            def _():
                that = dbuf.at[8, at + 1]
                remote(that, that, dt_s.at[0], dt_r.at[at], ring(1)).wait_recv()

    @pl.when(tm == 7)
    def _():
        pl.semaphore_wait(know.at[3], 3)

    def pass_old():
        return remote(oldv.at[0], oldv.at[1], f_s.at[4], f_r.at[4], (tm + 1, gz))

    def pass_fine(n):
        return remote(fab.at[0, 4 + n], fprev.at[n], f_s.at[n], f_r.at[n], (tm + 1, gz))

    def to_relay(n):
        return remote(fab.at[0, 4 + n], relay, rl_s.at[n], rl_r, (n + 3, gz))

    def from_relay(n):
        return remote(relay, fprev.at[n], rl_s.at[0], f_r.at[n], (8, gz))

    send(tm == 7, *[functools.partial(to_relay, n) for n in range(1, 4)], functools.partial(pass_fine, 0), pass_old)

    def dg_copy(j):
        i = j + 8 if j < 0 else j + 7
        some = pl.ds(0, min(5, 9 - abs(j)))
        return remote(dbuf.at[8, some], dbuf.at[8 - j, some], dg_s.at[i], dg_r.at[i], (tm, gz + j))

    def dl_copy(j):
        i = j + 3 if j < 0 else j + 2
        some = pl.ds(5, 4 - abs(j))
        return remote(dbuf.at[8, some], dbuf.at[8 - j, some], dl_s.at[i], dl_r.at[i], (tm, gz + j))

    @pl.when((tm > 0) & (tm < 8))
    def _():
        c0_copy(1).wait_recv()

    dt_here(0, 4)
    for j in around[::-1]:
        send(has(j), functools.partial(dg_copy, j))
    dt_here(4, 7)
    for j in around[:6][::-1]:
        send(has(j), functools.partial(dl_copy, j))
    for n in range(1, 4):

        @pl.when(tm == n + 3)
        def _():
            to_relay(n).wait_recv()

        send(tm == n + 3, functools.partial(from_relay, n))
    send((tm < NT - 1) & (tm != 7), pass_old, *[functools.partial(pass_fine, n) for n in range(4)])

    for j in around:

        @pl.when(has(-j))
        def _():
            gc_copy(j).wait_recv()

    sides, vertical, kept, heat = coarse_coefs(gbuf[:, 0], gbuf[1:16, 1], c0, [has(j) for j in range(-8, 9)])
    for i in range(4):
        cside[i] = sides[i]
    cz[...] = vertical
    ckeep[...] = kept
    chp[...] = heat

    def cr_copy(j):
        return remote(gs.at[9], c8.at[8 - j], cr_s.at[j + 7], cr_r.at[j + 7], (tm + 8, gz + j))

    def g8_copy():
        return remote(gs.at[8], gs.at[0], cr_s.at[15], cr_r.at[15], (8, gz))

    for j in around:

        @pl.when(has(-j))
        def _():
            dg_copy(j).wait_recv()

    for j in range(-7, 8):

        @pl.when(is_b & has(-j) & (zi >= abs(j)))
        def _():
            cr_copy(j).wait_recv()

    state[...] = jnp.where(is_b, c8[...], dbuf[:, 0])
    for s in range(1, 9):
        if s == 5:
            for j in around[:6]:

                @pl.when(has(-j))
                def _():
                    dl_copy(j).wait_recv()

        if s == 8:
            dt_here(7, 8)

        @pl.when(is_a | (zi >= s))
        def _():
            n = 17 - 2 * s
            lo = s - 1
            latest = coarse_step(
                state[pl.ds(lo, n + 2)],
                [cside[i, pl.ds(lo, n)] for i in range(4)],
                cz[pl.ds(lo, n)],
                cz[pl.ds(lo + 1, n)],
                ckeep[pl.ds(lo, n)],
                chp[pl.ds(lo, n)],
                gbuf[pl.ds(s, n), 2],
            )
            gs[s] = latest[8 - s]
            state[pl.ds(s, n)] = latest + dbuf[pl.ds(s, n), s]

    @pl.when(is_a)
    def _():
        gs[9] = state[8]

    @pl.when(tm != 7)
    def _():
        pl.semaphore_wait(know.at[3], 3)

    send(tm == 0, g8_copy)
    for j in sorted(range(-7, 8), key=lambda j: -abs(j)):
        send((tm < 8) & (zi >= abs(j)) & has(j), functools.partial(cr_copy, j))

    @pl.when(tm == 8)
    def _():
        g8_copy().wait_recv()

    @pl.when(tm > 0)
    def _():
        pass_old().wait_recv()
        for n in range(4):
            pass_fine(n).wait_recv()
        fine = unpool(gs[zi] - oldv[1])
        for n in range(4):
            out[n] = fprev[n] + fine

    finish()


def on_device(starts, materials, conductivity, pre_factor, activation):
    vmem, dma = pltpu.VMEM, pltpu.SemaphoreType.DMA
    slabs = vmem((12, 128, 128), F32)
    tile = lambda *lead: vmem(lead + (8, 128), F32)
    held = lambda x: pltpu.with_memory_space_constraint(x, pltpu.HBM)
    result = pl.pallas_call(
        kernel,
        name="parareal",
        out_shape=jax.ShapeDtypeStruct((4, 128, 128), F32),
        in_specs=[pl.BlockSpec(memory_space=pltpu.HBM)] * 2 + [pl.BlockSpec(memory_space=pltpu.SMEM)] * 3,
        out_specs=pl.BlockSpec(memory_space=pltpu.VMEM),
        scratch_shapes=[
            vmem((2, 12, 128, 128), F32),
            vmem((12, 128, 128), jnp.int32),
            *([slabs] * 9),
            vmem((4, 128, 128), F32),
            vmem((128, 128), F32),
            tile(2),
            tile(3, 2),
            tile(17, 3),
            tile(17, 9),
            tile(17),
            tile(17),
            tile(10),
            tile(16),
            tile(4, 15),
            tile(15),
            tile(15),
            dma((2,)),
            dma((2,)),
            dma((2,)),
            dma((2, 4, 2)),
            dma((2, 4, 2)),
            dma((7,)),
            dma(()),
            dma((16,)),
            dma((16,)),
            dma((7,)),
            dma((8,)),
            dma((16,)),
            dma((16,)),
            dma((6,)),
            dma((6,)),
            dma((16,)),
            dma((16,)),
            dma((5,)),
            dma((5,)),
            dma((4,)),
            dma(()),
            pltpu.SemaphoreType.REGULAR((4,)),
        ],
        compiler_params=pltpu.CompilerParams(
            collective_id=0, has_side_effects=True, vmem_limit_bytes=40 * 2**20
        ),
        cost_estimate=pl.CostEstimate(flops=50_000_000, bytes_accessed=2_000_000, transcendentals=500_000),
    )(held(starts[0]), held(materials), conductivity, pre_factor, activation)
    return result[None]


def solution(mesh):
    return jax.shard_map(
        on_device,
        mesh=mesh,
        in_specs=(P("tm", "gz", None, None), P("gz", None, None), P(), P(), P()),
        out_specs=P("tm", "gz", None, None),
        check_vma=False,
    )
```

time: 49.3 us -> 41.2 us (0.84)
  the two profiles are of different devices: /device:TPU:505 before, /device:TPU:48 now
where the time goes in v2:
time: 41.2 us; the launch traced here: 41.1 us
  Pallas kernels  39.7 us (96%)
  local copies, waits for them, and re-layouts  1.39 us (3%)
    pallas_call x1, Pallas kernels, on_device(): pl.pallas_call(kernel, name='parareal', out_shape=jax.ShapeDtypeStruct((4...  39.7 us
    unnamed x7, local copies, waits for them, and re-layouts  1.39 us

profile of v2, /device:TPU:48, one launch (start us, length us, event | category | flops | bytes accessed | tf_op | source)
XLA Modules:
  0.0 41.1 jit_solution(4848101940756718600)
XLA Ops:
  0.0 0.0 copy-start.2
  0.0 0.0 copy-start.1
  0.0 0.0 copy-start
  0.0 0.6 %copy-done.2 = f32[3]{0:T(128)S(1)} copy-done((f32[3]{0:T(128)S(1)}, f32[3]{0:T(128)}, u32[]{:S(2)}) %copy-start.2) | copy-done | bytes 36
  0.7 0.0 copy-done.1
  0.7 0.0 copy-done
  0.7 39.7 %parareal.1 = f32[4,128,128]{2,1,0:T(8,128)S(1)} custom-call(f32[4,128,128]{2,1,0:T(8,128)} %bitcast.3, s32[4,128,128]{2,1,0:T(8,128)} %materials.1, f32[3]{0:T(128)S(1)} %copy-done, f32[3]{0:T(128)S(1)} %copy-done.1, f32[3]{0:T(128)S(1)} %copy-done.2), custom_call_target="tpu_custom_call" | custom-call | flops 50000000 | bytes 2000000 | tf_op jit(solution)/shard_map/parareal/pallas_call | solution.py:569
  40.4 0.7 %copy.7 = f32[1,4,128,128]{3,2,1,0:T(8,128)} copy(f32[1,4,128,128]{3,2,1,0:T(8,128)S(1)} %bitcast.2) | data formatting | bytes 524288
Async XLA Ops:
  0.0 0.7 %copy-start.2 = (f32[3]{0:T(128)S(1)}, f32[3]{0:T(128)}, u32[]{:S(2)}) copy-start(f32[3]{0:T(128)} %act.1) | copy-start | bytes 40
  0.0 0.7 %copy-start.1 = (f32[3]{0:T(128)S(1)}, f32[3]{0:T(128)}, u32[]{:S(2)}) copy-start(f32[3]{0:T(128)} %pre.1) | copy-start | bytes 40
  0.0 0.7 %copy-start = (f32[3]{0:T(128)S(1)}, f32[3]{0:T(128)}, u32[]{:S(2)}) copy-start(f32[3]{0:T(128)} %cond.1) | copy-start | bytes 40

commit v3 on v2

--- a/solution.py
+++ b/solution.py
@@ -16,10 +16,6 @@
 NT = 16
 
 
-def dot(a, b):
-    return jnp.dot(a, b, precision=lax.Precision.HIGHEST, preferred_element_type=F32)
-
-
 def iota(shape, dim):
     return lax.broadcasted_iota(jnp.int32, shape, dim)
 
@@ -28,15 +24,30 @@
     return jnp.where(mask, F32(1.0), F32(0.0))
 
 
-def pool(totals):
-    n = len(totals)
+def lane_dot(x, weights):
+    high = x.astype(jnp.bfloat16)
+    left = x - high.astype(F32)
+    middle = left.astype(jnp.bfloat16)
+    low = (left - middle.astype(F32)).astype(jnp.bfloat16)
+    weights = weights.astype(jnp.bfloat16)
+    return jnp.dot(
+        jnp.concatenate([high, middle, low], axis=1),
+        jnp.concatenate([weights] * 3, axis=0),
+        preferred_element_type=F32,
+    )
+
+
+def pool(totals, rows):
     cols = ones_where(iota((128, 128), 0) // 4 == iota((128, 128), 1) % 32)
-    rows = ones_where(iota((32, 128), 0) == iota((32, 128), 1) // 4)
-    wide = dot(rows, jnp.concatenate(totals, axis=1))
-    tall = dot(jnp.concatenate([wide[:, 128 * i : 128 * i + 128] for i in range(n)], axis=0), cols)
+    parts = []
+    for i, total in enumerate(totals):
+        rows[i] = total
+        four = [rows[i, pl.ds(q, 32, stride=4)] for q in range(4)]
+        parts.append((four[0] + four[1]) + (four[2] + four[3]))
+    tall = lane_dot(jnp.concatenate(parts, axis=0), cols)
     group = iota((8, 128), 1) // 32
     outs = []
-    for i in range(n):
+    for i in range(len(totals)):
         out = jnp.zeros((8, 128), F32)
         for g in range(4):
             at = 32 * i + 8 * g
@@ -45,12 +56,12 @@
     return outs
 
 
-def unpool(coarse):
+def unpool(coarse, rows):
     group = iota((8, 128), 1) // 32
     u = jnp.concatenate([jnp.where(group == g, coarse, F32(0.0)) for g in range(4)], axis=0)
-    rows_t = ones_where(iota((128, 32), 0) // 4 == iota((128, 32), 1))
-    cols_t = ones_where(iota((128, 128), 0) % 32 == iota((128, 128), 1) // 4)
-    return dot(rows_t, dot(u, cols_t))
+    wide = lane_dot(u, ones_where(iota((128, 128), 0) % 32 == iota((128, 128), 1) // 4))
+    for q in range(4):
+        rows[pl.ds(q, 32, stride=4)] = wide
 
 
 def release(v, hp, act):
@@ -109,10 +120,14 @@
 def kernel(
     starts,
     materials,
+    cond_in,
+    pre_in,
+    act_in,
+    out,
     cond,
     pre,
     act,
-    out,
+    rows4,
     fab,
     ids,
     kbuf,
@@ -156,6 +171,7 @@
     cr_r,
     f_s,
     f_r,
+    st_r,
     rl_s,
     rl_r,
     know,
@@ -227,11 +243,17 @@
             n = n + has(j).astype(jnp.int32) + has_slice(j).astype(jnp.int32)
         pl.semaphore_wait(sem, n)
 
-    c0, is_b = cond[0], hi == 1
+    is_b = hi == 1
     is_a = jnp.logical_not(is_b)
 
     own_f = pltpu.make_async_copy(starts, fab.at[0, pl.ds(4, 4)], local_sem.at[0])
     own_m = pltpu.make_async_copy(materials, ids.at[pl.ds(4, 4)], local_sem.at[1])
+    tables = [
+        pltpu.make_async_copy(src, dst, local_sem.at[2 + i])
+        for i, (src, dst) in enumerate(((cond_in, cond), (pre_in, pre), (act_in, act)))
+    ]
+    for table in tables:
+        table.start()
     own_m.start()
     own_f.start()
     for j, at in ((-1, 0), (1, 8)):
@@ -243,13 +265,15 @@
 
     near[...] = jnp.zeros(near.shape, F32)
     gbuf[...] = jnp.zeros(gbuf.shape, F32)
-    gbuf[:, 0] = jnp.full((17, 8, 128), c0, F32)
     dbuf[...] = jnp.zeros(dbuf.shape, F32)
     c8[...] = jnp.zeros(c8.shape, F32)
 
     barrier = pltpu.get_barrier_semaphore()
     tell(barrier, 1)
 
+    for table in tables:
+        table.wait()
+    c0 = cond[0]
     own_m.wait()
     totals = [jnp.zeros((128, 128), F32) for _ in range(3)]
     for n in range(4):
@@ -257,7 +281,7 @@
         totals = [t + lookup(layer, table) for t, table in zip(totals, (cond, pre, act))]
     own_f.wait()
     totals.append(fab[0, 4] + fab[0, 5] + fab[0, 6] + fab[0, 7])
-    pooled = pool(totals)
+    pooled = pool(totals, rows4)
     for i in range(3):
         gbuf[8, i] = pooled[i]
     own_coarse = pooled[3]
@@ -329,15 +353,18 @@
         new = new + kyu[layer] * pltpu.roll(v, 127, 0) + kyd[layer] * pltpu.roll(v, 1, 0)
         fab[1 - at, layer] = new + release(v, hp[layer], actb[layer])
 
-    def slab_here(n):
+    def slab_here(n, what):
         for j in (1, -1):
 
             @pl.when(has(-j))
             def _():
-                slab(j, n, 1).wait_recv()
-                slab(j, n, 0).wait_recv()
+                slab(j, n, what).wait_recv()
 
     def stage(n):
+        if n > 0:
+            fine_step(5, n % 2)
+            fine_step(6, n % 2)
+        slab_here(n, 1)
         sources(3 - n)
         sources(8 + n)
         if n == 0:
@@ -350,14 +377,18 @@
         else:
             faces(4 - n)
             faces(7 + n)
+        slab_here(n, 0)
 
         def pair(i, _):
-            at = lax.rem(jnp.minimum(i, n), 2)
+            at = lax.rem(i, 2)
             fine_step(4 - n + i, at)
             fine_step(7 + n - i, at)
             return 0
 
-        lax.fori_loop(0, n + 2, pair, 0)
+        lax.fori_loop(0, n + 1, pair, 0)
+        if n == 0:
+            fine_step(5, 0)
+            fine_step(6, 0)
 
     def own_sources(i, _):
         sources(4 + i)
@@ -389,29 +420,61 @@
     hear(know.at[1], 2)
     tell(know.at[2], 4)
     for n in range(3):
-        slab_here(n)
         stage(n)
-    hear(know.at[2], 4)
-    tell_one(know.at[3], ygo(4))
-    tell_one(know.at[3], ring(1))
-    tell_one(know.at[3], ring(-1))
-
-    def c0_copy(n):
-        return remote(dbuf.at[8, 0], dbuf.at[8, 0], c0_s.at[n - 1], c0_r, (n, gz))
-
-    send(tm == 0, *[functools.partial(c0_copy, n) for n in range(1, 8)])
-    slab_here(3)
 
     def gc_copy(j):
         i = j + 8 if j < 0 else j + 7
         return remote(gbuf.at[8], gbuf.at[8 - j], gc_s.at[i], gc_r.at[i], (tm, gz + j))
 
+    def c0_copy(n):
+        return remote(dbuf.at[8, 0], dbuf.at[8, 0], c0_s.at[n - 1], c0_r, (n, gz))
+
     around = [j for d in range(1, 9) for j in (d, -d)]
-    for j in around:
-        send(has(j), functools.partial(gc_copy, j))
-
+
+    def coarse_out(when):
+        @pl.when(when)
+        def _():
+            hear(know.at[2], 4)
+            tell_one(know.at[3], ygo(4))
+            tell_one(know.at[3], ring(1))
+            tell_one(know.at[3], ring(-1))
+
+        for j in around:
+            send(when & has(j), functools.partial(gc_copy, j))
+
+    late = zi >= 4
+    coarse_out(late)
     stage(3)
-    dbuf[8, zi + 1] = pool([fab[0, 4] + fab[0, 5] + fab[0, 6] + fab[0, 7]])[0] - old
+
+    def pass_old():
+        return remote(oldv.at[0], oldv.at[1], f_s.at[4], f_r.at[4], (tm + 1, gz))
+
+    def pass_fine(n):
+        return remote(fab.at[0, 4 + n], fprev.at[n], f_s.at[n], f_r.at[n], (tm + 1, gz))
+
+    def pass_strip(n):
+        strip = pl.ds(0, 32)
+        return remote(fab.at[0, 4 + n, strip], fprev.at[n, strip], f_s.at[n], st_r.at[n - 1], (8, gz))
+
+    def to_relay(n):
+        return remote(fab.at[0, 4 + n, pl.ds(32, 96)], relay, rl_s.at[n], rl_r, (n + 3, gz))
+
+    def from_relay(n):
+        return remote(relay, fprev.at[n, pl.ds(32, 96)], rl_s.at[0], f_r.at[n], (8, gz))
+
+    send(tm == 7, *[functools.partial(to_relay, n) for n in range(1, 4)])
+
+    @pl.when(tm == 7)
+    def _():
+        pl.semaphore_wait(know.at[3], 3)
+
+    send(
+        tm == 7, functools.partial(pass_fine, 0), *[functools.partial(pass_strip, n) for n in range(1, 4)], pass_old
+    )
+    dbuf[8, zi + 1] = pool([fab[0, 4] + fab[0, 5] + fab[0, 6] + fab[0, 7]], rows4)[0] - old
+    coarse_out(jnp.logical_not(late))
+
+    send(tm == 0, *[functools.partial(c0_copy, n) for n in range(1, 8)])
 
     def dt_copy(k):
         own = dbuf.at[8, zi + 1]
@@ -427,23 +490,8 @@
                 that = dbuf.at[8, at + 1]
                 remote(that, that, dt_s.at[0], dt_r.at[at], ring(1)).wait_recv()
 
-    @pl.when(tm == 7)
-    def _():
-        pl.semaphore_wait(know.at[3], 3)
-
-    def pass_old():
-        return remote(oldv.at[0], oldv.at[1], f_s.at[4], f_r.at[4], (tm + 1, gz))
-
-    def pass_fine(n):
-        return remote(fab.at[0, 4 + n], fprev.at[n], f_s.at[n], f_r.at[n], (tm + 1, gz))
-
-    def to_relay(n):
-        return remote(fab.at[0, 4 + n], relay, rl_s.at[n], rl_r, (n + 3, gz))
-
-    def from_relay(n):
-        return remote(relay, fprev.at[n], rl_s.at[0], f_r.at[n], (8, gz))
-
-    send(tm == 7, *[functools.partial(to_relay, n) for n in range(1, 4)], functools.partial(pass_fine, 0), pass_old)
+    whole = [pass_old] + [functools.partial(pass_fine, n) for n in range(4)]
+    send(zi < 2, *whole)
 
     def dg_copy(j):
         i = j + 8 if j < 0 else j + 7
@@ -462,17 +510,17 @@
     dt_here(0, 4)
     for j in around[::-1]:
         send(has(j), functools.partial(dg_copy, j))
+    for n in range(1, 4):
+
+        @pl.when(tm == n + 3)
+        def _():
+            to_relay(n).wait_recv()
+
+        send(tm == n + 3, functools.partial(from_relay, n))
     dt_here(4, 7)
     for j in around[:6][::-1]:
         send(has(j), functools.partial(dl_copy, j))
-    for n in range(1, 4):
-
-        @pl.when(tm == n + 3)
-        def _():
-            to_relay(n).wait_recv()
-
-        send(tm == n + 3, functools.partial(from_relay, n))
-    send((tm < NT - 1) & (tm != 7), pass_old, *[functools.partial(pass_fine, n) for n in range(4)])
+    send((zi >= 2) & (zi < 7), *whole)
 
     for j in around:
 
@@ -480,7 +528,10 @@
         def _():
             gc_copy(j).wait_recv()
 
-    sides, vertical, kept, heat = coarse_coefs(gbuf[:, 0], gbuf[1:16, 1], c0, [has(j) for j in range(-8, 9)])
+    k_all = jnp.concatenate(
+        [jnp.where(has(j), gbuf[j + 8 : j + 9, 0], c0) for j in range(-8, 9)], axis=0
+    )
+    sides, vertical, kept, heat = coarse_coefs(k_all, gbuf[1:16, 1], c0, [has(j) for j in range(-8, 9)])
     for i in range(4):
         cside[i] = sides[i]
     cz[...] = vertical
@@ -552,9 +603,21 @@
     @pl.when(tm > 0)
     def _():
         pass_old().wait_recv()
-        for n in range(4):
-            pass_fine(n).wait_recv()
-        fine = unpool(gs[zi] - oldv[1])
+        unpool(gs[zi] - oldv[1], rows4.at[0])
+
+        @pl.when(tm != 8)
+        def _():
+            for n in range(4):
+                pass_fine(n).wait_recv()
+
+        @pl.when(tm == 8)
+        def _():
+            pass_fine(0).wait_recv()
+            for n in range(1, 4):
+                pass_strip(n).wait_recv()
+                from_relay(n).wait_recv()
+
+        fine = rows4[0]
         for n in range(4):
             out[n] = fprev[n] + fine
 
@@ -570,14 +633,16 @@
         kernel,
         name="parareal",
         out_shape=jax.ShapeDtypeStruct((4, 128, 128), F32),
-        in_specs=[pl.BlockSpec(memory_space=pltpu.HBM)] * 2 + [pl.BlockSpec(memory_space=pltpu.SMEM)] * 3,
+        in_specs=[pl.BlockSpec(memory_space=pltpu.HBM)] * 5,
         out_specs=pl.BlockSpec(memory_space=pltpu.VMEM),
         scratch_shapes=[
+            *([pltpu.SMEM((3,), F32)] * 3),
+            vmem((4, 128, 128), F32),
             vmem((2, 12, 128, 128), F32),
             vmem((12, 128, 128), jnp.int32),
             *([slabs] * 9),
             vmem((4, 128, 128), F32),
-            vmem((128, 128), F32),
+            vmem((96, 128), F32),
             tile(2),
             tile(3, 2),
             tile(17, 3),
@@ -589,7 +654,7 @@
             tile(4, 15),
             tile(15),
             tile(15),
-            dma((2,)),
+            dma((5,)),
             dma((2,)),
             dma((2,)),
             dma((2, 4, 2)),
@@ -608,6 +673,7 @@
             dma((16,)),
             dma((5,)),
             dma((5,)),
+            dma((3,)),
             dma((4,)),
             dma(()),
             pltpu.SemaphoreType.REGULAR((4,)),
@@ -616,7 +682,7 @@
             collective_id=0, has_side_effects=True, vmem_limit_bytes=40 * 2**20
         ),
         cost_estimate=pl.CostEstimate(flops=50_000_000, bytes_accessed=2_000_000, transcendentals=500_000),
-    )(held(starts[0]), held(materials), conductivity, pre_factor, activation)
+    )(held(starts[0]), held(materials), held(conductivity), held(pre_factor), held(activation))
     return result[None]
 
 

time: 41.2 us -> 37 us (0.90)
  the two profiles are of different devices: /device:TPU:48 before, /device:TPU:56 now
where the time goes in v3:
time: 37 us; the launch traced here: 36.9 us
  Pallas kernels  36.2 us (98%)
  local copies, waits for them, and re-layouts  0.71 us (2%)
    pallas_call x1, Pallas kernels, on_device(): pl.pallas_call(kernel, name='parareal', out_shape=jax.ShapeDtypeStruct((4...  36.2 us

profile of v3, /device:TPU:56, one launch (start us, length us, event | category | flops | bytes accessed | tf_op | source)
XLA Modules:
  0.0 36.9 jit_solution(4926477862200712449)
XLA Ops:
  0.0 36.2 %parareal.1 = f32[4,128,128]{2,1,0:T(8,128)S(1)} custom-call(f32[4,128,128]{2,1,0:T(8,128)} %bitcast.3, s32[4,128,128]{2,1,0:T(8,128)} %materials.1, f32[3]{0:T(128)} %cond_in.1, f32[3]{0:T(128)} %pre_in.1, f32[3]{0:T(128)} %act_in.1), custom_call_target="tpu_custom_call" | custom-call | flops 50000000 | bytes 2000000 | tf_op jit(solution)/shard_map/parareal/pallas_call | solution.py:632
  36.2 0.7 %copy.7 = f32[1,4,128,128]{3,2,1,0:T(8,128)} copy(f32[1,4,128,128]{3,2,1,0:T(8,128)S(1)} %bitcast.2) | data formatting | bytes 524288

commit v4 on v3

--- a/solution.py
+++ b/solution.py
@@ -141,6 +141,7 @@
     actb,
     fprev,
     relay,
+    ownd,
     oldv,
     near,
     gbuf,
@@ -171,7 +172,7 @@
     cr_r,
     f_s,
     f_r,
-    st_r,
+    part_r,
     rl_s,
     rl_r,
     know,
@@ -246,6 +247,8 @@
     is_b = hi == 1
     is_a = jnp.logical_not(is_b)
 
+    barrier = pltpu.get_barrier_semaphore()
+    tell(barrier, 1)
     own_f = pltpu.make_async_copy(starts, fab.at[0, pl.ds(4, 4)], local_sem.at[0])
     own_m = pltpu.make_async_copy(materials, ids.at[pl.ds(4, 4)], local_sem.at[1])
     tables = [
@@ -256,20 +259,22 @@
         table.start()
     own_m.start()
     own_f.start()
+
     for j, at in ((-1, 0), (1, 8)):
 
         @pl.when(jnp.logical_not(has(j)))
         def _():
             fab[0, pl.ds(at, 4)] = jnp.zeros((4, 128, 128), F32)
             ids[pl.ds(at, 4)] = jnp.zeros((4, 128, 128), jnp.int32)
-
-    near[...] = jnp.zeros(near.shape, F32)
-    gbuf[...] = jnp.zeros(gbuf.shape, F32)
-    dbuf[...] = jnp.zeros(dbuf.shape, F32)
-    c8[...] = jnp.zeros(c8.shape, F32)
-
-    barrier = pltpu.get_barrier_semaphore()
-    tell(barrier, 1)
+            near[1 + j] = jnp.zeros((2, 8, 128), F32)
+
+    for j in range(-8, 9):
+
+        @pl.when(jnp.logical_not(has(j)))
+        def _():
+            gbuf[8 + j] = jnp.zeros((3, 8, 128), F32)
+            dbuf[8 + j] = jnp.zeros((9, 8, 128), F32)
+            c8[8 + j] = jnp.zeros((8, 128), F32)
 
     for table in tables:
         table.wait()
@@ -452,46 +457,80 @@
     def pass_fine(n):
         return remote(fab.at[0, 4 + n], fprev.at[n], f_s.at[n], f_r.at[n], (tm + 1, gz))
 
-    def pass_strip(n):
-        strip = pl.ds(0, 32)
-        return remote(fab.at[0, 4 + n, strip], fprev.at[n, strip], f_s.at[n], st_r.at[n - 1], (8, gz))
-
-    def to_relay(n):
-        return remote(fab.at[0, 4 + n, pl.ds(32, 96)], relay, rl_s.at[n], rl_r, (n + 3, gz))
-
-    def from_relay(n):
-        return remote(relay, fprev.at[n, pl.ds(32, 96)], rl_s.at[0], f_r.at[n], (8, gz))
-
-    send(tm == 7, *[functools.partial(to_relay, n) for n in range(1, 4)])
-
-    @pl.when(tm == 7)
+    straight = ((1, 112, 16), (2, 112, 16), (3, 112, 16))
+
+    def pass_part(i):
+        layer, first, count = straight[i]
+        part = pl.ds(first, count)
+        return remote(fab.at[0, 4 + layer, part], fprev.at[layer, part], f_s.at[1 + i], part_r.at[4 + i], (8, gz))
+
+    ways = ((1, 0, 112), (2, 0, 112), (3, 0, 112))
+    by = (0, 6, 5)
+
+    def to_relay(i):
+        layer, first, count = ways[i]
+        return remote(
+            fab.at[0, 4 + layer, pl.ds(first, count)], relay.at[pl.ds(0, count)], rl_s.at[i], rl_r, (by[i], gz)
+        )
+
+    def from_relay(i):
+        layer, first, count = ways[i]
+        return remote(
+            relay.at[pl.ds(0, count)], fprev.at[layer, pl.ds(first, count)], rl_s.at[5], part_r.at[i], (8, gz)
+        )
+
+    def relay_on(i):
+        @pl.when(tm == by[i])
+        def _():
+            to_relay(i).wait_recv()
+
+        send(tm == by[i], functools.partial(from_relay, i))
+
+    def c0_here(when):
+        @pl.when(when)
+        def _():
+            c0_copy(1).wait_recv()
+
+    send(tm == 7, *[functools.partial(to_relay, i) for i in range(len(ways))])
+    c0_here(tm == 7)
+    parts = [functools.partial(pass_part, i) for i in range(len(straight))]
+    send(tm == 7, functools.partial(pass_fine, 0), *parts, pass_old)
+    ownd[0] = pool([fab[0, 4] + fab[0, 5] + fab[0, 6] + fab[0, 7]], rows4)[0] - old
+
+    eight = tm == 8
+
+    @pl.when(jnp.logical_not(eight))
     def _():
-        pl.semaphore_wait(know.at[3], 3)
-
-    send(
-        tm == 7, functools.partial(pass_fine, 0), *[functools.partial(pass_strip, n) for n in range(1, 4)], pass_old
-    )
-    dbuf[8, zi + 1] = pool([fab[0, 4] + fab[0, 5] + fab[0, 6] + fab[0, 7]], rows4)[0] - old
+        dbuf[8, zi + 1] = ownd[0]
+
     coarse_out(jnp.logical_not(late))
 
-    send(tm == 0, *[functools.partial(c0_copy, n) for n in range(1, 8)])
+    send(tm == 0, *[functools.partial(c0_copy, n) for n in range(1, 9)])
 
     def dt_copy(k):
-        own = dbuf.at[8, zi + 1]
-        return remote(own, own, dt_s.at[k - 1], dt_r.at[zi], ring(k))
-
-    send(tm >= 0, *[functools.partial(dt_copy, k) for k in (4, 3, 5, 2, 6, 1, 7)])
-
-    def dt_here(first, last):
+        return remote(ownd.at[0], dbuf.at[8, zi + 1], dt_s.at[k - 1], dt_r.at[zi], ring(k))
+
+    def d8_copy():
+        return remote(ownd.at[0], dbuf.at[8, zi + 1], dt_s.at[7], dt_r.at[zi], (8, gz))
+
+    send(tm < 5, d8_copy)
+    for k in (4, 3, 5, 2, 6, 1, 7):
+        send(jnp.logical_not(is_b & (lax.rem(zi + k, 8) == 0)), functools.partial(dt_copy, k))
+
+    def dt_here(first, last, when):
         for at in range(first, last):
 
-            @pl.when(zi != at)
+            @pl.when(when & (jnp.logical_not(eight) & (zi != at) if at == 7 else eight | (zi != at)))
             def _():
                 that = dbuf.at[8, at + 1]
                 remote(that, that, dt_s.at[0], dt_r.at[at], ring(1)).wait_recv()
 
     whole = [pass_old] + [functools.partial(pass_fine, n) for n in range(4)]
     send(zi < 2, *whole)
+
+    asks = (tm == 5) | (tm == 6)
+    dt_here(0, 1, asks)
+    send(asks, d8_copy)
 
     def dg_copy(j):
         i = j + 8 if j < 0 else j + 7
@@ -503,21 +542,15 @@
         some = pl.ds(5, 4 - abs(j))
         return remote(dbuf.at[8, some], dbuf.at[8 - j, some], dl_s.at[i], dl_r.at[i], (tm, gz + j))
 
-    @pl.when((tm > 0) & (tm < 8))
-    def _():
-        c0_copy(1).wait_recv()
-
-    dt_here(0, 4)
+    c0_here((tm > 0) & (tm <= 8) & (tm != 7))
+
+    dt_here(0, 1, jnp.logical_not(asks))
+    dt_here(1, 4, tm >= 0)
     for j in around[::-1]:
         send(has(j), functools.partial(dg_copy, j))
-    for n in range(1, 4):
-
-        @pl.when(tm == n + 3)
-        def _():
-            to_relay(n).wait_recv()
-
-        send(tm == n + 3, functools.partial(from_relay, n))
-    dt_here(4, 7)
+    for i in range(len(ways)):
+        relay_on(i)
+    dt_here(4, 7, tm >= 0)
     for j in around[:6][::-1]:
         send(has(j), functools.partial(dl_copy, j))
     send((zi >= 2) & (zi < 7), *whole)
@@ -541,9 +574,6 @@
     def cr_copy(j):
         return remote(gs.at[9], c8.at[8 - j], cr_s.at[j + 7], cr_r.at[j + 7], (tm + 8, gz + j))
 
-    def g8_copy():
-        return remote(gs.at[8], gs.at[0], cr_s.at[15], cr_r.at[15], (8, gz))
-
     for j in around:
 
         @pl.when(has(-j))
@@ -552,11 +582,11 @@
 
     for j in range(-7, 8):
 
-        @pl.when(is_b & has(-j) & (zi >= abs(j)))
+        @pl.when((tm > 8) & has(-j) & (zi >= abs(j)))
         def _():
             cr_copy(j).wait_recv()
 
-    state[...] = jnp.where(is_b, c8[...], dbuf[:, 0])
+    state[...] = jnp.where(tm > 8, c8[...], dbuf[:, 0])
     for s in range(1, 9):
         if s == 5:
             for j in around[:6]:
@@ -566,9 +596,9 @@
                     dl_copy(j).wait_recv()
 
         if s == 8:
-            dt_here(7, 8)
-
-        @pl.when(is_a | (zi >= s))
+            dt_here(7, 8, tm >= 0)
+
+        @pl.when((tm <= 8) | (zi >= s))
         def _():
             n = 17 - 2 * s
             lo = s - 1
@@ -588,22 +618,14 @@
     def _():
         gs[9] = state[8]
 
-    @pl.when(tm != 7)
-    def _():
-        pl.semaphore_wait(know.at[3], 3)
-
-    send(tm == 0, g8_copy)
+    pl.semaphore_wait(know.at[3], 3)
     for j in sorted(range(-7, 8), key=lambda j: -abs(j)):
-        send((tm < 8) & (zi >= abs(j)) & has(j), functools.partial(cr_copy, j))
-
-    @pl.when(tm == 8)
-    def _():
-        g8_copy().wait_recv()
+        send((tm > 0) & (tm < 8) & (zi >= abs(j)) & has(j), functools.partial(cr_copy, j))
 
     @pl.when(tm > 0)
     def _():
         pass_old().wait_recv()
-        unpool(gs[zi] - oldv[1], rows4.at[0])
+        unpool(gs[jnp.where(eight, 8, zi)] - oldv[1], rows4.at[0])
 
         @pl.when(tm != 8)
         def _():
@@ -613,9 +635,10 @@
         @pl.when(tm == 8)
         def _():
             pass_fine(0).wait_recv()
-            for n in range(1, 4):
-                pass_strip(n).wait_recv()
-                from_relay(n).wait_recv()
+            for i in range(len(straight)):
+                pass_part(i).wait_recv()
+            for i in range(len(ways)):
+                from_relay(i).wait_recv()
 
         fine = rows4[0]
         for n in range(4):
@@ -642,7 +665,8 @@
             vmem((12, 128, 128), jnp.int32),
             *([slabs] * 9),
             vmem((4, 128, 128), F32),
-            vmem((96, 128), F32),
+            vmem((128, 128), F32),
+            tile(1),
             tile(2),
             tile(3, 2),
             tile(17, 3),
@@ -659,11 +683,11 @@
             dma((2,)),
             dma((2, 4, 2)),
             dma((2, 4, 2)),
-            dma((7,)),
+            dma((8,)),
             dma(()),
             dma((16,)),
             dma((16,)),
-            dma((7,)),
+            dma((8,)),
             dma((8,)),
             dma((16,)),
             dma((16,)),
@@ -673,8 +697,8 @@
             dma((16,)),
             dma((5,)),
             dma((5,)),
-            dma((3,)),
-            dma((4,)),
+            dma((8,)),
+            dma((6,)),
             dma(()),
             pltpu.SemaphoreType.REGULAR((4,)),
         ],

time: 37 us -> 35.9 us (0.970)
  Pallas kernels: 36.2 us -> 34.8 us
    pallas_call x1, Pallas kernels: 36.2 us -> 34.8 us  [on_device(): pl.pallas_call(kernel, name='parareal', out_shape=jax.ShapeDtypeStruct((4...]
where the time goes in v4:
time: 35.9 us; the launch traced here: 35.5 us
  Pallas kernels  34.8 us (97%)
  local copies, waits for them, and re-layouts  0.71 us (2%)
    pallas_call x1, Pallas kernels, on_device(): pl.pallas_call(kernel, name='parareal', out_shape=jax.ShapeDtypeStruct((4...  34.8 us

profile of v4, /device:TPU:56, one launch (start us, length us, event | category | flops | bytes accessed | tf_op | source)
XLA Modules:
  0.0 35.5 jit_solution(18038811192795162369)
XLA Ops:
  0.0 34.8 %parareal.1 = f32[4,128,128]{2,1,0:T(8,128)S(1)} custom-call(f32[4,128,128]{2,1,0:T(8,128)} %bitcast.3, s32[4,128,128]{2,1,0:T(8,128)} %materials.1, f32[3]{0:T(128)} %cond_in.1, f32[3]{0:T(128)} %pre_in.1, f32[3]{0:T(128)} %act_in.1), custom_call_target="tpu_custom_call" | custom-call | flops 50000000 | bytes 2000000 | tf_op jit(solution)/shard_map/parareal/pallas_call | solution.py:655
  34.8 0.7 %copy.7 = f32[1,4,128,128]{3,2,1,0:T(8,128)} copy(f32[1,4,128,128]{3,2,1,0:T(8,128)S(1)} %bitcast.2) | data formatting | bytes 524288

commit v5 on v4

--- a/solution.py
+++ b/solution.py
@@ -166,6 +166,8 @@
     dt_r,
     dg_s,
     dg_r,
+    dm_s,
+    dm_r,
     dl_s,
     dl_r,
     cr_s,
@@ -358,6 +360,13 @@
         new = new + kyu[layer] * pltpu.roll(v, 127, 0) + kyd[layer] * pltpu.roll(v, 1, 0)
         fab[1 - at, layer] = new + release(v, hp[layer], actb[layer])
 
+    def fine_part(layer, inner, below):
+        v = fab[0, layer]
+        new = v * keep[layer] + kz[below] * fab[0, inner]
+        new = new + kxr[layer] * pltpu.roll(v, 127, 1) + kxl[layer] * pltpu.roll(v, 1, 1)
+        new = new + kyu[layer] * pltpu.roll(v, 127, 0) + kyd[layer] * pltpu.roll(v, 1, 0)
+        fab[1, layer] = new + release(v, hp[layer], actb[layer])
+
     def slab_here(n, what):
         for j in (1, -1):
 
@@ -382,7 +391,12 @@
         else:
             faces(4 - n)
             faces(7 + n)
+        low, high = 4 - n, 7 + n
+        fine_part(low, low + 1, low)
+        fine_part(high, high - 1, high - 1)
         slab_here(n, 0)
+        fab[1, low] = fab[1, low] + kz[low - 1] * fab[0, low - 1]
+        fab[1, high] = fab[1, high] + kz[high] * fab[0, high + 1]
 
         def pair(i, _):
             at = lax.rem(i, 2)
@@ -390,8 +404,9 @@
             fine_step(7 + n - i, at)
             return 0
 
-        lax.fori_loop(0, n + 1, pair, 0)
-        if n == 0:
+        if n > 0:
+            lax.fori_loop(1, n + 1, pair, 0)
+        else:
             fine_step(5, 0)
             fine_step(6, 0)
 
@@ -445,7 +460,7 @@
             tell_one(know.at[3], ring(-1))
 
         for j in around:
-            send(when & has(j), functools.partial(gc_copy, j))
+            send(when & (tm != 8) & has(j), functools.partial(gc_copy, j))
 
     late = zi >= 4
     coarse_out(late)
@@ -457,14 +472,14 @@
     def pass_fine(n):
         return remote(fab.at[0, 4 + n], fprev.at[n], f_s.at[n], f_r.at[n], (tm + 1, gz))
 
-    straight = ((1, 112, 16), (2, 112, 16), (3, 112, 16))
+    straight = ((2, 72, 56), (3, 72, 56))
 
     def pass_part(i):
         layer, first, count = straight[i]
         part = pl.ds(first, count)
         return remote(fab.at[0, 4 + layer, part], fprev.at[layer, part], f_s.at[1 + i], part_r.at[4 + i], (8, gz))
 
-    ways = ((1, 0, 112), (2, 0, 112), (3, 0, 112))
+    ways = ((1, 0, 128), (2, 0, 72), (3, 0, 72))
     by = (0, 6, 5)
 
     def to_relay(i):
@@ -498,29 +513,29 @@
     ownd[0] = pool([fab[0, 4] + fab[0, 5] + fab[0, 6] + fab[0, 7]], rows4)[0] - old
 
     eight = tm == 8
-
-    @pl.when(jnp.logical_not(eight))
-    def _():
-        dbuf[8, zi + 1] = ownd[0]
-
-    coarse_out(jnp.logical_not(late))
-
-    send(tm == 0, *[functools.partial(c0_copy, n) for n in range(1, 9)])
+    dbuf[8, zi + 1] = ownd[0]
 
     def dt_copy(k):
         return remote(ownd.at[0], dbuf.at[8, zi + 1], dt_s.at[k - 1], dt_r.at[zi], ring(k))
 
-    def d8_copy():
-        return remote(ownd.at[0], dbuf.at[8, zi + 1], dt_s.at[7], dt_r.at[zi], (8, gz))
-
-    send(tm < 5, d8_copy)
-    for k in (4, 3, 5, 2, 6, 1, 7):
-        send(jnp.logical_not(is_b & (lax.rem(zi + k, 8) == 0)), functools.partial(dt_copy, k))
-
-    def dt_here(first, last, when):
-        for at in range(first, last):
-
-            @pl.when(when & (jnp.logical_not(eight) & (zi != at) if at == 7 else eight | (zi != at)))
+    def dt_out(when):
+        for k in (4, 3, 5, 2, 6, 1, 7):
+            to = lax.rem(zi + k, 8)
+            skip = is_b & (to == 0)
+            send(when(to) & jnp.logical_not(skip), functools.partial(dt_copy, k))
+
+    early = jnp.logical_not(late)
+    send(tm == 0, *[functools.partial(c0_copy, n) for n in range(1, 5)])
+    dt_out(lambda to: early & (to <= zi + 4))
+
+    coarse_out(early)
+    send(tm == 0, *[functools.partial(c0_copy, n) for n in range(5, 8)])
+    dt_out(lambda to: late | (to > zi + 4))
+    def dt_here(first, end):
+        for at in range(first, end):
+            go = jnp.logical_not(eight) & (zi != at)
+
+            @pl.when(go)
             def _():
                 that = dbuf.at[8, at + 1]
                 remote(that, that, dt_s.at[0], dt_r.at[at], ring(1)).wait_recv()
@@ -528,36 +543,40 @@
     whole = [pass_old] + [functools.partial(pass_fine, n) for n in range(4)]
     send(zi < 2, *whole)
 
-    asks = (tm == 5) | (tm == 6)
-    dt_here(0, 1, asks)
-    send(asks, d8_copy)
-
     def dg_copy(j):
         i = j + 8 if j < 0 else j + 7
-        some = pl.ds(0, min(5, 9 - abs(j)))
+        some = pl.ds(0, min(3, 9 - abs(j)))
         return remote(dbuf.at[8, some], dbuf.at[8 - j, some], dg_s.at[i], dg_r.at[i], (tm, gz + j))
+
+    def dm_copy(j):
+        i = j + 5 if j < 0 else j + 4
+        some = pl.ds(3, min(2, 6 - abs(j)))
+        return remote(dbuf.at[8, some], dbuf.at[8 - j, some], dm_s.at[i], dm_r.at[i], (tm, gz + j))
 
     def dl_copy(j):
         i = j + 3 if j < 0 else j + 2
         some = pl.ds(5, 4 - abs(j))
         return remote(dbuf.at[8, some], dbuf.at[8 - j, some], dl_s.at[i], dl_r.at[i], (tm, gz + j))
 
-    c0_here((tm > 0) & (tm <= 8) & (tm != 7))
-
-    dt_here(0, 1, jnp.logical_not(asks))
-    dt_here(1, 4, tm >= 0)
+    c0_here((tm > 0) & (tm < 7))
+
+    dt_here(0, 2)
     for j in around[::-1]:
-        send(has(j), functools.partial(dg_copy, j))
+        send((tm != 8) & has(j), functools.partial(dg_copy, j))
+    dt_here(2, 4)
+    for j in around[:10][::-1]:
+        send((tm != 8) & has(j), functools.partial(dm_copy, j))
     for i in range(len(ways)):
         relay_on(i)
-    dt_here(4, 7, tm >= 0)
+    dt_here(4, 7)
+    relayed = jnp.logical_not(eight)
     for j in around[:6][::-1]:
-        send(has(j), functools.partial(dl_copy, j))
+        send(relayed & has(j), functools.partial(dl_copy, j))
     send((zi >= 2) & (zi < 7), *whole)
 
     for j in around:
 
-        @pl.when(has(-j))
+        @pl.when((tm != 8) & has(-j))
         def _():
             gc_copy(j).wait_recv()
 
@@ -576,7 +595,7 @@
 
     for j in around:
 
-        @pl.when(has(-j))
+        @pl.when((tm != 8) & has(-j))
         def _():
             dg_copy(j).wait_recv()
 
@@ -588,17 +607,24 @@
 
     state[...] = jnp.where(tm > 8, c8[...], dbuf[:, 0])
     for s in range(1, 9):
+        if s == 3:
+            for j in around[:10]:
+
+                @pl.when((tm != 8) & has(-j))
+                def _():
+                    dm_copy(j).wait_recv()
+
         if s == 5:
             for j in around[:6]:
 
-                @pl.when(has(-j))
+                @pl.when(relayed & has(-j))
                 def _():
                     dl_copy(j).wait_recv()
 
         if s == 8:
-            dt_here(7, 8, tm >= 0)
-
-        @pl.when((tm <= 8) | (zi >= s))
+            dt_here(7, 8)
+
+        @pl.when((tm < 8) | (zi >= s))
         def _():
             n = 17 - 2 * s
             lo = s - 1
@@ -618,14 +644,23 @@
     def _():
         gs[9] = state[8]
 
+    def g8_copy():
+        return remote(gs.at[8], gs.at[0], cr_s.at[15], cr_r.at[15], (8, gz))
+
+    send(tm == 0, g8_copy)
+
     pl.semaphore_wait(know.at[3], 3)
     for j in sorted(range(-7, 8), key=lambda j: -abs(j)):
         send((tm > 0) & (tm < 8) & (zi >= abs(j)) & has(j), functools.partial(cr_copy, j))
 
+    @pl.when(eight)
+    def _():
+        g8_copy().wait_recv()
+
     @pl.when(tm > 0)
     def _():
         pass_old().wait_recv()
-        unpool(gs[jnp.where(eight, 8, zi)] - oldv[1], rows4.at[0])
+        unpool(gs[zi] - oldv[1], rows4.at[0])
 
         @pl.when(tm != 8)
         def _():
@@ -691,6 +726,8 @@
             dma((8,)),
             dma((16,)),
             dma((16,)),
+            dma((10,)),
+            dma((10,)),
             dma((6,)),
             dma((6,)),
             dma((16,)),

time: 35.9 us -> 38.1 us (1.061)
  Pallas kernels: 34.8 us -> 37.3 us
    pallas_call x1, Pallas kernels: 34.8 us -> 37.3 us  [on_device(): pl.pallas_call(kernel, name='parareal', out_shape=jax.ShapeDtypeStruct((4...]
where the time goes in v5:
time: 38.1 us; the launch traced here: 38 us
  Pallas kernels  37.3 us (98%)
  local copies, waits for them, and re-layouts  0.71 us (2%)
    pallas_call x1, Pallas kernels, on_device(): pl.pallas_call(kernel, name='parareal', out_shape=jax.ShapeDtypeStruct((4...  37.3 us

profile of v5, /device:TPU:56, one launch (start us, length us, event | category | flops | bytes accessed | tf_op | source)
XLA Modules:
  0.0 38.0 jit_solution(10455490025792710944)
XLA Ops:
  0.0 37.3 %parareal.1 = f32[4,128,128]{2,1,0:T(8,128)S(1)} custom-call(f32[4,128,128]{2,1,0:T(8,128)} %bitcast.3, s32[4,128,128]{2,1,0:T(8,128)} %materials.1, f32[3]{0:T(128)} %cond_in.1, f32[3]{0:T(128)} %pre_in.1, f32[3]{0:T(128)} %act_in.1), custom_call_target="tpu_custom_call" | custom-call | flops 50000000 | bytes 2000000 | tf_op jit(solution)/shard_map/parareal/pallas_call | solution.py:690
  37.3 0.7 %copy.7 = f32[1,4,128,128]{3,2,1,0:T(8,128)} copy(f32[1,4,128,128]{3,2,1,0:T(8,128)S(1)} %bitcast.2) | data formatting | bytes 524288
